TPU v7x, 128 devices: a whole 4x4x4 slice. The times are simulated.
128 devices in a mesh: slab: 16 (over y, x), sub: 8 (over z, core).
Axes of the slice: x: 4, y: 4, z: 4, core: 2. Of those that a mesh axis runs over, the one named last changes fastest.
Arguments:
- ref_pos: float32 [3, 1048576], P(None, ('slab', 'sub')), may hold values from 0 to 1
- disp: float32 [3, 1048576], P(None, ('slab', 'sub')), may hold values from -0.3 to 0.3
- vel: float32 [3, 1048576], P(None, ('slab', 'sub')), may hold values from -0.6 to 0.6
- pressure: float32 [1024, 1024], P('slab', 'sub'), may hold values from 0.2 to 1.5
- conductivity: float32 [1024, 1024], P('slab', 'sub'), may hold values from 0.02 to 0.2
- frac_mask: int32 [1024, 1024], P('slab', 'sub'), may hold values 0 or 1
- send_list: int32 [2048, 32], P(('slab', 'sub')), may hold values from 0 to 63
- pair_list: int32 [32768, 2], P(('slab', 'sub')), may hold values from 0 to 511
- pair_count: int32 [128], P(('slab', 'sub')), may hold values from 128 to 256, as said below
- bond_flags: int32 [32768, 10, 128], P(('slab', 'sub')), may hold values from 0 to 16383, as said below
Outputs:
- disp_out: float32 [3, 1048576], P(None, ('slab', 'sub'))
- vel_out: float32 [3, 1048576], P(None, ('slab', 'sub'))
- pressure_out: float32 [1024, 1024], P('slab', 'sub')
Inputs may be any that keep to these rules, and one draw needn't show every extreme that they name: send_list entries are local block numbers of the sending device; pair_list entries number received copies as sender position * 32 + slot. `pair_count`: one device in every draw holds exactly 256 live pair slots. `bond_flags`: the flag of bond (a, b) is bit a % 14 of word a // 14 in column b; bits beyond 128 rows are zero.
All inputs are finite; a program needn't handle non-finite values. No bound on the sum of `frac_mask` on one device may be relied on, other than what follows from the above.
Results may differ from a plain program's by a relative error of at most 0.0003.
Values sent between devices are 32-bit elements; how exact they have to be, the bound alone decides.
A program may use at most 64 MiB of HBM per device.

v0:
```python
import math

import jax
import jax.numpy as jnp
from jax import lax
from jax.sharding import PartitionSpec as P

STEPS = 2


soft_sq = 0.0025
reach_sq = 0.09
stiffness = 4.0
pressure_coupling = 0.3
time_step = 0.2
flow_step = 1.0


def extended(cells, sides, width):
    for axis, dim in sides:
        count = lax.axis_size(axis)
        ends = count - 1
        head = lax.slice_in_dim(cells, 0, width, axis=dim)
        tail = lax.slice_in_dim(cells, cells.shape[dim] - width, cells.shape[dim], axis=dim)
        cells = jnp.concatenate(
            [
                lax.ppermute(tail, axis, [(i, (i + 1) % count) for i in range(ends)]),
                cells,
                lax.ppermute(head, axis, [((i + 1) % count, i) for i in range(ends)]),
            ],
            axis=dim,
        )
    return cells


def unpack_flags(packed, width):
    shifts = jnp.arange(14, dtype=jnp.int32)
    spread = jnp.bitwise_and(jnp.right_shift(packed[:, :, None, :], shifts[None, None, :, None]), 1)
    spread = spread.reshape(packed.shape[0], packed.shape[1] * 14, packed.shape[2])
    return spread[:, :width, :].astype(jnp.float32)


def tile_forces(start_first, start_second, moving_first, moving_second, packed, alive):
    offset = start_second[:, :, None, :] - start_first[:, :, :, None]
    stretched = offset + moving_second[:3, :, None, :] - moving_first[:3, :, :, None]
    rest_sq = jnp.sum(offset * offset, axis=0)
    rest_len = jnp.sqrt(rest_sq + soft_sq)
    now_len = jnp.sqrt(jnp.sum(stretched * stretched, axis=0) + soft_sq)
    influence = reach_sq / (reach_sq + rest_sq)
    mean_pressure = 0.5 * (moving_first[3][:, :, None] + moving_second[3][:, None, :])
    flags = unpack_flags(packed, offset.shape[-1])
    factor = (
        stiffness
        * flags
        * alive[:, None, None]
        * influence
        * ((now_len - rest_len) / rest_len - pressure_coupling * mean_pressure)
        / now_len
    )
    bond_force = factor[None] * stretched
    return (jnp.sum(bond_force, axis=3), -jnp.sum(bond_force, axis=2))


def flow(centre, padded, wet, conduct, rock):
    total = jnp.zeros_like(centre)
    for shift_row, shift_col in ((1, 0), (-1, 0), (0, 1), (0, -1)):
        rows = slice(1 + shift_row, padded.shape[0] - 1 + shift_row)
        cols = slice(1 + shift_col, padded.shape[1] - 1 + shift_col)
        face = 0.5 * (conduct * wet * rock[0, rows, cols] + rock[1, rows, cols] * wet)
        total = total + face * (padded[rows, cols] - centre)
    return centre + flow_step * total


def body(
    ref_pos,
    disp,
    vel,
    pressure,
    conductivity,
    frac_mask,
    send_list,
    pair_list,
    pair_count,
    bond_flags,
):
    points = disp.shape[1]
    width = bond_flags.shape[2]
    blocks = points // width
    peers = lax.axis_size("slab")
    capacity = send_list.shape[1]
    slots = peers * capacity
    pair_total = pair_list.shape[0]
    group = math.gcd(pair_total, 32)
    outgoing = send_list.reshape(-1)
    owner_table = (outgoing[None, :] == jnp.arange(blocks, dtype=jnp.int32)[:, None]).astype(
        jnp.float32
    )
    slot_range = jnp.arange(slots, dtype=jnp.int32)[None, :]
    first_table = (pair_list[:, 0:1] == slot_range).astype(jnp.float32)
    second_table = (pair_list[:, 1:2] == slot_range).astype(jnp.float32)
    live = (jnp.arange(pair_total, dtype=jnp.int32) < pair_count[0]).astype(jnp.float32)
    wet = frac_mask.astype(jnp.float32)
    rock = extended(jnp.stack([wet, conductivity * wet]), (("slab", 1), ("sub", 2)), 1)

    def select(field, table):
        return jnp.einsum("csp,ks->ckp", field, table, precision=lax.Precision.HIGHEST)

    for step_index in range(STEPS):
        wet_points = (pressure * wet).reshape(1, points)
        outbound_field = jnp.concatenate([ref_pos, disp, wet_points], axis=0)
        shaped = outbound_field.reshape(outbound_field.shape[0], blocks, width)
        chosen = jnp.einsum("cbp,bs->csp", shaped, owner_table, precision=lax.Precision.HIGHEST)
        arrived = lax.all_to_all(
            chosen.reshape(outbound_field.shape[0], peers, capacity, width),
            "slab",
            split_axis=1,
            concat_axis=1,
            tiled=True,
        ).reshape(7, slots, width)
        start_slots = arrived[:3]
        moving_slots = arrived[3:]
        start_first = select(start_slots, first_table)
        start_second = select(start_slots, second_table)
        moving_first = select(moving_slots, first_table)
        moving_second = select(moving_slots, second_table)

        def one_group(index):

            def cut(field):
                return lax.dynamic_slice_in_dim(field, index * group, group, 1)

            packed = lax.dynamic_slice_in_dim(bond_flags, index * group, group, 0)
            alive = lax.dynamic_slice_in_dim(live, index * group, group, 0)
            return tile_forces(
                cut(start_first),
                cut(start_second),
                cut(moving_first),
                cut(moving_second),
                packed,
                alive,
            )

        on_first, on_second = lax.map(one_group, jnp.arange(pair_total // group, dtype=jnp.int32))
        on_first = on_first.transpose(1, 0, 2, 3).reshape(3, pair_total, width)
        on_second = on_second.transpose(1, 0, 2, 3).reshape(3, pair_total, width)
        slot_force = jnp.einsum(
            "ckp,ks->csp", on_first, first_table, precision=lax.Precision.HIGHEST
        )
        slot_force = slot_force + jnp.einsum(
            "ckp,ks->csp", on_second, second_table, precision=lax.Precision.HIGHEST
        )
        returned = lax.all_to_all(
            slot_force.reshape(3, peers, capacity, width),
            "slab",
            split_axis=1,
            concat_axis=1,
            tiled=True,
        ).reshape(3, slots, width)
        force = jnp.einsum(
            "csp,bs->cbp", returned, owner_table, precision=lax.Precision.HIGHEST
        ).reshape(3, points)
        padded = extended(pressure, (("slab", 0), ("sub", 1)), 1)
        pressure = flow(pressure, padded, wet, conductivity, rock)
        vel = vel + time_step * force
        disp = disp + time_step * vel
    return (disp, vel, pressure)


def solution(mesh):
    in_specs = (
        P(None, ("slab", "sub")),
        P(None, ("slab", "sub")),
        P(None, ("slab", "sub")),
        P("slab", "sub"),
        P("slab", "sub"),
        P("slab", "sub"),
        P(("slab", "sub"), None),
        P(("slab", "sub"), None),
        P(("slab", "sub")),
        P(("slab", "sub"), None, None),
    )
    out_specs = (P(None, ("slab", "sub")), P(None, ("slab", "sub")), P("slab", "sub"))
    return jax.shard_map(body, mesh=mesh, in_specs=in_specs, out_specs=out_specs, check_vma=False)
```

profile of v0, /device:TPU:96, one launch (start us, length us, event | category | flops | bytes accessed | tf_op | source)
XLA Modules:
  0.0 528.1 jit_solution(8743165420336743778)
XLA Ops:
  6.5 7.2 %all-to-all-start = ((f32[7,16,32,128]{3,2,0,1:T(8,128)}), f32[7,16,32,128]{3,2,0,1:T(8,128)S(1)}, u32[]{:S(2)}, u32[]{:S(2)}) async-start(f32[7,16,32,128]{3,2,0,1:T(8,128)} %copy.103), calls=%async_computation | async-start | bytes 3670016 | tf_op jit(solution)/shard_map/all_to_all | solution.py:113
  15.5 5.1 collective-permute-start.2
  22.0 4.5 collective-permute-start.3
  27.2 10.6 %collective-permute-done.1 = f32[1,128]{1,0:T(1,128)S(1)} collective-permute-done((f32[1,128]{1,0:T(1,128)S(1)}, f32[1,128]{1,0:T(1,128)S(1)}, u32[]{:S(2)}, u32[]{:S(2)}) %collective-permute-start.1) | collective-permute-done | bytes 544 | tf_op jit(solution)/shard_map/ppermute | solution.py:29
  46.4 196.5 %while.28 = (s32[]{:T(128)}, f32[8,3,32,128]{3,2,0,1:T(8,128)S(1)}, f32[8,3,32,128]{3,2,0,1:T(8,128)S(1)}, s32[8]{0:T(128)S(1)}, s32[256,10,128]{2,0,1:T(8,128)}...) while((s32[]{:T(128)}, f32[8,3,32,128]{3,2,0,1:T(8,128)S(1)}, ...), condition=%wide.region_5.6_spmd, body=%wide.region_0.5_spmd.sunk | while | flops 27775016 | bytes 29167488 | solution.py:143
  49.5 6.2 %fusion.158 = (f32[32,128,128]{2,1,0:T(8,128)}, f32[32,128,128]{2,1,0:T(8,128)}) fusion(f32[3,32,128]{2,1,0:T(8,128)S(1)} %constant_dynamic-slice_fusion.25, f32[3,32,128]{2,1,0:T(8,128)S(1)} %constant_dynamic-slice_fusion.26, f32[3,32,128]{2,1,0:T(8,128)S(1)} %constant_dynamic-slice_fusion.27, f32[3,32,128]{2,1,0:T(8,128)S(1)} %constant_dynamic-slice_fusion.28), kind=kLoop, calls=%fused_computation.2.clone.1 | loop fusion | flops 9961472 | bytes 4390912 | tf_op jit(solution)/shard_map/while/body/eval_jaxpr/reduce_sum | solution.py:46
  58.6 5.1 fusion.159
  64.9 6.0 %fusion.160 = (f32[3,32,128]{2,1,0:T(8,128)S(1)}, f32[3,32,128]{2,1,0:T(8,128)S(1)}) fusion(f32[32,128,128]{2,1,0:T(8,128)S(1)} %copy.203, f32[3,32,128]{2,1,0:T(8,128)S(1)} %constant_dynamic-slice_fusion.27, f32[3,32,128]{2,1,0:T(8,128)S(1)} %constant_dynamic-slice_fusion.28, f32[3,32,128]{2,1,0:T(8,128)S(1)} %constant_dynamic-slice_fusion.25, ...), kind=kLoop, calls=%fused_computation.6.clone.1 | loop fusion | flops 9412608 | bytes 2392064 | tf_op jit(solution)/shard_map/while/body/eval_jaxpr/reduce_sum | solution.py:61
  74.1 6.2 %fusion.158 = (f32[32,128,128]{2,1,0:T(8,128)}, f32[32,128,128]{2,1,0:T(8,128)}) fusion(f32[3,32,128]{2,1,0:T(8,128)S(1)} %constant_dynamic-slice_fusion.25, f32[3,32,128]{2,1,0:T(8,128)S(1)} %constant_dynamic-slice_fusion.26, f32[3,32,128]{2,1,0:T(8,128)S(1)} %constant_dynamic-slice_fusion.27, f32[3,32,128]{2,1,0:T(8,128)S(1)} %constant_dynamic-slice_fusion.28), kind=kLoop, calls=%fused_computation.2.clone.1 | loop fusion | flops 9961472 | bytes 4390912 | tf_op jit(solution)/shard_map/while/body/eval_jaxpr/reduce_sum | solution.py:46
  83.2 5.1 fusion.159
  89.5 6.0 %fusion.160 = (f32[3,32,128]{2,1,0:T(8,128)S(1)}, f32[3,32,128]{2,1,0:T(8,128)S(1)}) fusion(f32[32,128,128]{2,1,0:T(8,128)S(1)} %copy.203, f32[3,32,128]{2,1,0:T(8,128)S(1)} %constant_dynamic-slice_fusion.27, f32[3,32,128]{2,1,0:T(8,128)S(1)} %constant_dynamic-slice_fusion.28, f32[3,32,128]{2,1,0:T(8,128)S(1)} %constant_dynamic-slice_fusion.25, ...), kind=kLoop, calls=%fused_computation.6.clone.1 | loop fusion | flops 9412608 | bytes 2392064 | tf_op jit(solution)/shard_map/while/body/eval_jaxpr/reduce_sum | solution.py:61
  98.6 6.2 %fusion.158 = (f32[32,128,128]{2,1,0:T(8,128)}, f32[32,128,128]{2,1,0:T(8,128)}) fusion(f32[3,32,128]{2,1,0:T(8,128)S(1)} %constant_dynamic-slice_fusion.25, f32[3,32,128]{2,1,0:T(8,128)S(1)} %constant_dynamic-slice_fusion.26, f32[3,32,128]{2,1,0:T(8,128)S(1)} %constant_dynamic-slice_fusion.27, f32[3,32,128]{2,1,0:T(8,128)S(1)} %constant_dynamic-slice_fusion.28), kind=kLoop, calls=%fused_computation.2.clone.1 | loop fusion | flops 9961472 | bytes 4390912 | tf_op jit(solution)/shard_map/while/body/eval_jaxpr/reduce_sum | solution.py:46
  107.7 5.1 fusion.159
  114.0 6.0 %fusion.160 = (f32[3,32,128]{2,1,0:T(8,128)S(1)}, f32[3,32,128]{2,1,0:T(8,128)S(1)}) fusion(f32[32,128,128]{2,1,0:T(8,128)S(1)} %copy.203, f32[3,32,128]{2,1,0:T(8,128)S(1)} %constant_dynamic-slice_fusion.27, f32[3,32,128]{2,1,0:T(8,128)S(1)} %constant_dynamic-slice_fusion.28, f32[3,32,128]{2,1,0:T(8,128)S(1)} %constant_dynamic-slice_fusion.25, ...), kind=kLoop, calls=%fused_computation.6.clone.1 | loop fusion | flops 9412608 | bytes 2392064 | tf_op jit(solution)/shard_map/while/body/eval_jaxpr/reduce_sum | solution.py:61
  123.2 6.2 %fusion.158 = (f32[32,128,128]{2,1,0:T(8,128)}, f32[32,128,128]{2,1,0:T(8,128)}) fusion(f32[3,32,128]{2,1,0:T(8,128)S(1)} %constant_dynamic-slice_fusion.25, f32[3,32,128]{2,1,0:T(8,128)S(1)} %constant_dynamic-slice_fusion.26, f32[3,32,128]{2,1,0:T(8,128)S(1)} %constant_dynamic-slice_fusion.27, f32[3,32,128]{2,1,0:T(8,128)S(1)} %constant_dynamic-slice_fusion.28), kind=kLoop, calls=%fused_computation.2.clone.1 | loop fusion | flops 9961472 | bytes 4390912 | tf_op jit(solution)/shard_map/while/body/eval_jaxpr/reduce_sum | solution.py:46
  132.3 5.1 fusion.159
  138.6 6.0 %fusion.160 = (f32[3,32,128]{2,1,0:T(8,128)S(1)}, f32[3,32,128]{2,1,0:T(8,128)S(1)}) fusion(f32[32,128,128]{2,1,0:T(8,128)S(1)} %copy.203, f32[3,32,128]{2,1,0:T(8,128)S(1)} %constant_dynamic-slice_fusion.27, f32[3,32,128]{2,1,0:T(8,128)S(1)} %constant_dynamic-slice_fusion.28, f32[3,32,128]{2,1,0:T(8,128)S(1)} %constant_dynamic-slice_fusion.25, ...), kind=kLoop, calls=%fused_computation.6.clone.1 | loop fusion | flops 9412608 | bytes 2392064 | tf_op jit(solution)/shard_map/while/body/eval_jaxpr/reduce_sum | solution.py:61
  147.7 6.2 %fusion.158 = (f32[32,128,128]{2,1,0:T(8,128)}, f32[32,128,128]{2,1,0:T(8,128)}) fusion(f32[3,32,128]{2,1,0:T(8,128)S(1)} %constant_dynamic-slice_fusion.25, f32[3,32,128]{2,1,0:T(8,128)S(1)} %constant_dynamic-slice_fusion.26, f32[3,32,128]{2,1,0:T(8,128)S(1)} %constant_dynamic-slice_fusion.27, f32[3,32,128]{2,1,0:T(8,128)S(1)} %constant_dynamic-slice_fusion.28), kind=kLoop, calls=%fused_computation.2.clone.1 | loop fusion | flops 9961472 | bytes 4390912 | tf_op jit(solution)/shard_map/while/body/eval_jaxpr/reduce_sum | solution.py:46
  156.8 5.1 fusion.159
  163.1 6.0 %fusion.160 = (f32[3,32,128]{2,1,0:T(8,128)S(1)}, f32[3,32,128]{2,1,0:T(8,128)S(1)}) fusion(f32[32,128,128]{2,1,0:T(8,128)S(1)} %copy.203, f32[3,32,128]{2,1,0:T(8,128)S(1)} %constant_dynamic-slice_fusion.27, f32[3,32,128]{2,1,0:T(8,128)S(1)} %constant_dynamic-slice_fusion.28, f32[3,32,128]{2,1,0:T(8,128)S(1)} %constant_dynamic-slice_fusion.25, ...), kind=kLoop, calls=%fused_computation.6.clone.1 | loop fusion | flops 9412608 | bytes 2392064 | tf_op jit(solution)/shard_map/while/body/eval_jaxpr/reduce_sum | solution.py:61
  172.3 6.2 %fusion.158 = (f32[32,128,128]{2,1,0:T(8,128)}, f32[32,128,128]{2,1,0:T(8,128)}) fusion(f32[3,32,128]{2,1,0:T(8,128)S(1)} %constant_dynamic-slice_fusion.25, f32[3,32,128]{2,1,0:T(8,128)S(1)} %constant_dynamic-slice_fusion.26, f32[3,32,128]{2,1,0:T(8,128)S(1)} %constant_dynamic-slice_fusion.27, f32[3,32,128]{2,1,0:T(8,128)S(1)} %constant_dynamic-slice_fusion.28), kind=kLoop, calls=%fused_computation.2.clone.1 | loop fusion | flops 9961472 | bytes 4390912 | tf_op jit(solution)/shard_map/while/body/eval_jaxpr/reduce_sum | solution.py:46
  181.4 5.1 fusion.159
  187.7 6.0 %fusion.160 = (f32[3,32,128]{2,1,0:T(8,128)S(1)}, f32[3,32,128]{2,1,0:T(8,128)S(1)}) fusion(f32[32,128,128]{2,1,0:T(8,128)S(1)} %copy.203, f32[3,32,128]{2,1,0:T(8,128)S(1)} %constant_dynamic-slice_fusion.27, f32[3,32,128]{2,1,0:T(8,128)S(1)} %constant_dynamic-slice_fusion.28, f32[3,32,128]{2,1,0:T(8,128)S(1)} %constant_dynamic-slice_fusion.25, ...), kind=kLoop, calls=%fused_computation.6.clone.1 | loop fusion | flops 9412608 | bytes 2392064 | tf_op jit(solution)/shard_map/while/body/eval_jaxpr/reduce_sum | solution.py:61
  196.8 6.2 %fusion.158 = (f32[32,128,128]{2,1,0:T(8,128)}, f32[32,128,128]{2,1,0:T(8,128)}) fusion(f32[3,32,128]{2,1,0:T(8,128)S(1)} %constant_dynamic-slice_fusion.25, f32[3,32,128]{2,1,0:T(8,128)S(1)} %constant_dynamic-slice_fusion.26, f32[3,32,128]{2,1,0:T(8,128)S(1)} %constant_dynamic-slice_fusion.27, f32[3,32,128]{2,1,0:T(8,128)S(1)} %constant_dynamic-slice_fusion.28), kind=kLoop, calls=%fused_computation.2.clone.1 | loop fusion | flops 9961472 | bytes 4390912 | tf_op jit(solution)/shard_map/while/body/eval_jaxpr/reduce_sum | solution.py:46
  205.9 5.1 fusion.159
  212.3 6.0 %fusion.160 = (f32[3,32,128]{2,1,0:T(8,128)S(1)}, f32[3,32,128]{2,1,0:T(8,128)S(1)}) fusion(f32[32,128,128]{2,1,0:T(8,128)S(1)} %copy.203, f32[3,32,128]{2,1,0:T(8,128)S(1)} %constant_dynamic-slice_fusion.27, f32[3,32,128]{2,1,0:T(8,128)S(1)} %constant_dynamic-slice_fusion.28, f32[3,32,128]{2,1,0:T(8,128)S(1)} %constant_dynamic-slice_fusion.25, ...), kind=kLoop, calls=%fused_computation.6.clone.1 | loop fusion | flops 9412608 | bytes 2392064 | tf_op jit(solution)/shard_map/while/body/eval_jaxpr/reduce_sum | solution.py:61
  221.4 6.2 %fusion.158 = (f32[32,128,128]{2,1,0:T(8,128)}, f32[32,128,128]{2,1,0:T(8,128)}) fusion(f32[3,32,128]{2,1,0:T(8,128)S(1)} %constant_dynamic-slice_fusion.25, f32[3,32,128]{2,1,0:T(8,128)S(1)} %constant_dynamic-slice_fusion.26, f32[3,32,128]{2,1,0:T(8,128)S(1)} %constant_dynamic-slice_fusion.27, f32[3,32,128]{2,1,0:T(8,128)S(1)} %constant_dynamic-slice_fusion.28), kind=kLoop, calls=%fused_computation.2.clone.1 | loop fusion | flops 9961472 | bytes 4390912 | tf_op jit(solution)/shard_map/while/body/eval_jaxpr/reduce_sum | solution.py:46
  230.5 5.1 fusion.159
  236.8 6.0 %fusion.160 = (f32[3,32,128]{2,1,0:T(8,128)S(1)}, f32[3,32,128]{2,1,0:T(8,128)S(1)}) fusion(f32[32,128,128]{2,1,0:T(8,128)S(1)} %copy.203, f32[3,32,128]{2,1,0:T(8,128)S(1)} %constant_dynamic-slice_fusion.27, f32[3,32,128]{2,1,0:T(8,128)S(1)} %constant_dynamic-slice_fusion.28, f32[3,32,128]{2,1,0:T(8,128)S(1)} %constant_dynamic-slice_fusion.25, ...), kind=kLoop, calls=%fused_computation.6.clone.1 | loop fusion | flops 9412608 | bytes 2392064 | tf_op jit(solution)/shard_map/while/body/eval_jaxpr/reduce_sum | solution.py:61
  245.2 3.8 all-to-all-start.1
  254.3 3.2 collective-permute-start.5
  259.6 3.2 collective-permute-done.7
  267.5 7.2 %all-to-all-start.2 = ((f32[7,16,32,128]{3,2,0,1:T(8,128)}), f32[7,16,32,128]{3,2,0,1:T(8,128)S(1)}, u32[]{:S(2)}, u32[]{:S(2)}) async-start(f32[7,16,32,128]{3,2,0,1:T(8,128)} %copy.115), calls=%async_computation.2 | async-start | bytes 3670016 | tf_op jit(solution)/shard_map/all_to_all | solution.py:113
  274.7 24.6 %all-to-all-done.2 = f32[7,16,32,128]{3,2,0,1:T(8,128)S(1)} async-done(((f32[7,16,32,128]{3,2,0,1:T(8,128)}), f32[7,16,32,128]{3,2,0,1:T(8,128)S(1)}, u32[]{:S(2)}, u32[]{:S(2)}) %all-to-all-start.2) | async-done | bytes 1835040 | tf_op jit(solution)/shard_map/all_to_all | solution.py:113
  304.2 196.9 %while.29 = (s32[]{:T(128)}, f32[8,3,32,128]{3,2,0,1:T(8,128)S(1)}, f32[8,3,32,128]{3,2,0,1:T(8,128)S(1)}, s32[8]{0:T(128)S(1)}, s32[256,10,128]{2,0,1:T(8,128)}...) while((s32[]{:T(128)}, f32[8,3,32,128]{3,2,0,1:T(8,128)S(1)}, ...), condition=%wide.region_11.12_spmd, body=%wide.region_6.11_spmd.sunk | while | flops 27775016 | bytes 29167488 | solution.py:143
  307.3 6.2 %fusion.161 = (f32[32,128,128]{2,1,0:T(8,128)}, f32[32,128,128]{2,1,0:T(8,128)}) fusion(f32[3,32,128]{2,1,0:T(8,128)S(1)} %constant_dynamic-slice_fusion.31, f32[3,32,128]{2,1,0:T(8,128)S(1)} %constant_dynamic-slice_fusion.32, f32[3,32,128]{2,1,0:T(8,128)S(1)} %constant_dynamic-slice_fusion.33, f32[3,32,128]{2,1,0:T(8,128)S(1)} %constant_dynamic-slice_fusion.34), kind=kLoop, calls=%fused_computation.32.clone.1 | loop fusion | flops 9961472 | bytes 4390912 | tf_op jit(solution)/shard_map/while/body/eval_jaxpr/reduce_sum | solution.py:46
  316.4 5.1 fusion.162
  322.7 6.0 %fusion.163 = (f32[3,32,128]{2,1,0:T(8,128)S(1)}, f32[3,32,128]{2,1,0:T(8,128)S(1)}) fusion(f32[32,128,128]{2,1,0:T(8,128)S(1)} %copy.207, f32[3,32,128]{2,1,0:T(8,128)S(1)} %constant_dynamic-slice_fusion.33, f32[3,32,128]{2,1,0:T(8,128)S(1)} %constant_dynamic-slice_fusion.34, f32[3,32,128]{2,1,0:T(8,128)S(1)} %constant_dynamic-slice_fusion.31, ...), kind=kLoop, calls=%fused_computation.36.clone.1 | loop fusion | flops 9412608 | bytes 2392064 | tf_op jit(solution)/shard_map/while/body/eval_jaxpr/reduce_sum | solution.py:61
  331.9 6.2 %fusion.161 = (f32[32,128,128]{2,1,0:T(8,128)}, f32[32,128,128]{2,1,0:T(8,128)}) fusion(f32[3,32,128]{2,1,0:T(8,128)S(1)} %constant_dynamic-slice_fusion.31, f32[3,32,128]{2,1,0:T(8,128)S(1)} %constant_dynamic-slice_fusion.32, f32[3,32,128]{2,1,0:T(8,128)S(1)} %constant_dynamic-slice_fusion.33, f32[3,32,128]{2,1,0:T(8,128)S(1)} %constant_dynamic-slice_fusion.34), kind=kLoop, calls=%fused_computation.32.clone.1 | loop fusion | flops 9961472 | bytes 4390912 | tf_op jit(solution)/shard_map/while/body/eval_jaxpr/reduce_sum | solution.py:46
  341.0 5.1 fusion.162
  347.3 6.0 %fusion.163 = (f32[3,32,128]{2,1,0:T(8,128)S(1)}, f32[3,32,128]{2,1,0:T(8,128)S(1)}) fusion(f32[32,128,128]{2,1,0:T(8,128)S(1)} %copy.207, f32[3,32,128]{2,1,0:T(8,128)S(1)} %constant_dynamic-slice_fusion.33, f32[3,32,128]{2,1,0:T(8,128)S(1)} %constant_dynamic-slice_fusion.34, f32[3,32,128]{2,1,0:T(8,128)S(1)} %constant_dynamic-slice_fusion.31, ...), kind=kLoop, calls=%fused_computation.36.clone.1 | loop fusion | flops 9412608 | bytes 2392064 | tf_op jit(solution)/shard_map/while/body/eval_jaxpr/reduce_sum | solution.py:61
  356.5 6.2 %fusion.161 = (f32[32,128,128]{2,1,0:T(8,128)}, f32[32,128,128]{2,1,0:T(8,128)}) fusion(f32[3,32,128]{2,1,0:T(8,128)S(1)} %constant_dynamic-slice_fusion.31, f32[3,32,128]{2,1,0:T(8,128)S(1)} %constant_dynamic-slice_fusion.32, f32[3,32,128]{2,1,0:T(8,128)S(1)} %constant_dynamic-slice_fusion.33, f32[3,32,128]{2,1,0:T(8,128)S(1)} %constant_dynamic-slice_fusion.34), kind=kLoop, calls=%fused_computation.32.clone.1 | loop fusion | flops 9961472 | bytes 4390912 | tf_op jit(solution)/shard_map/while/body/eval_jaxpr/reduce_sum | solution.py:46
  365.6 5.1 fusion.162
  371.9 6.0 %fusion.163 = (f32[3,32,128]{2,1,0:T(8,128)S(1)}, f32[3,32,128]{2,1,0:T(8,128)S(1)}) fusion(f32[32,128,128]{2,1,0:T(8,128)S(1)} %copy.207, f32[3,32,128]{2,1,0:T(8,128)S(1)} %constant_dynamic-slice_fusion.33, f32[3,32,128]{2,1,0:T(8,128)S(1)} %constant_dynamic-slice_fusion.34, f32[3,32,128]{2,1,0:T(8,128)S(1)} %constant_dynamic-slice_fusion.31, ...), kind=kLoop, calls=%fused_computation.36.clone.1 | loop fusion | flops 9412608 | bytes 2392064 | tf_op jit(solution)/shard_map/while/body/eval_jaxpr/reduce_sum | solution.py:61
  381.1 6.2 %fusion.161 = (f32[32,128,128]{2,1,0:T(8,128)}, f32[32,128,128]{2,1,0:T(8,128)}) fusion(f32[3,32,128]{2,1,0:T(8,128)S(1)} %constant_dynamic-slice_fusion.31, f32[3,32,128]{2,1,0:T(8,128)S(1)} %constant_dynamic-slice_fusion.32, f32[3,32,128]{2,1,0:T(8,128)S(1)} %constant_dynamic-slice_fusion.33, f32[3,32,128]{2,1,0:T(8,128)S(1)} %constant_dynamic-slice_fusion.34), kind=kLoop, calls=%fused_computation.32.clone.1 | loop fusion | flops 9961472 | bytes 4390912 | tf_op jit(solution)/shard_map/while/body/eval_jaxpr/reduce_sum | solution.py:46
  390.2 5.1 fusion.162
  396.5 6.0 %fusion.163 = (f32[3,32,128]{2,1,0:T(8,128)S(1)}, f32[3,32,128]{2,1,0:T(8,128)S(1)}) fusion(f32[32,128,128]{2,1,0:T(8,128)S(1)} %copy.207, f32[3,32,128]{2,1,0:T(8,128)S(1)} %constant_dynamic-slice_fusion.33, f32[3,32,128]{2,1,0:T(8,128)S(1)} %constant_dynamic-slice_fusion.34, f32[3,32,128]{2,1,0:T(8,128)S(1)} %constant_dynamic-slice_fusion.31, ...), kind=kLoop, calls=%fused_computation.36.clone.1 | loop fusion | flops 9412608 | bytes 2392064 | tf_op jit(solution)/shard_map/while/body/eval_jaxpr/reduce_sum | solution.py:61
  405.7 6.2 %fusion.161 = (f32[32,128,128]{2,1,0:T(8,128)}, f32[32,128,128]{2,1,0:T(8,128)}) fusion(f32[3,32,128]{2,1,0:T(8,128)S(1)} %constant_dynamic-slice_fusion.31, f32[3,32,128]{2,1,0:T(8,128)S(1)} %constant_dynamic-slice_fusion.32, f32[3,32,128]{2,1,0:T(8,128)S(1)} %constant_dynamic-slice_fusion.33, f32[3,32,128]{2,1,0:T(8,128)S(1)} %constant_dynamic-slice_fusion.34), kind=kLoop, calls=%fused_computation.32.clone.1 | loop fusion | flops 9961472 | bytes 4390912 | tf_op jit(solution)/shard_map/while/body/eval_jaxpr/reduce_sum | solution.py:46
  414.8 5.1 fusion.162
  421.2 6.0 %fusion.163 = (f32[3,32,128]{2,1,0:T(8,128)S(1)}, f32[3,32,128]{2,1,0:T(8,128)S(1)}) fusion(f32[32,128,128]{2,1,0:T(8,128)S(1)} %copy.207, f32[3,32,128]{2,1,0:T(8,128)S(1)} %constant_dynamic-slice_fusion.33, f32[3,32,128]{2,1,0:T(8,128)S(1)} %constant_dynamic-slice_fusion.34, f32[3,32,128]{2,1,0:T(8,128)S(1)} %constant_dynamic-slice_fusion.31, ...), kind=kLoop, calls=%fused_computation.36.clone.1 | loop fusion | flops 9412608 | bytes 2392064 | tf_op jit(solution)/shard_map/while/body/eval_jaxpr/reduce_sum | solution.py:61
  430.4 6.2 %fusion.161 = (f32[32,128,128]{2,1,0:T(8,128)}, f32[32,128,128]{2,1,0:T(8,128)}) fusion(f32[3,32,128]{2,1,0:T(8,128)S(1)} %constant_dynamic-slice_fusion.31, f32[3,32,128]{2,1,0:T(8,128)S(1)} %constant_dynamic-slice_fusion.32, f32[3,32,128]{2,1,0:T(8,128)S(1)} %constant_dynamic-slice_fusion.33, f32[3,32,128]{2,1,0:T(8,128)S(1)} %constant_dynamic-slice_fusion.34), kind=kLoop, calls=%fused_computation.32.clone.1 | loop fusion | flops 9961472 | bytes 4390912 | tf_op jit(solution)/shard_map/while/body/eval_jaxpr/reduce_sum | solution.py:46
  439.5 5.1 fusion.162
  445.8 6.0 %fusion.163 = (f32[3,32,128]{2,1,0:T(8,128)S(1)}, f32[3,32,128]{2,1,0:T(8,128)S(1)}) fusion(f32[32,128,128]{2,1,0:T(8,128)S(1)} %copy.207, f32[3,32,128]{2,1,0:T(8,128)S(1)} %constant_dynamic-slice_fusion.33, f32[3,32,128]{2,1,0:T(8,128)S(1)} %constant_dynamic-slice_fusion.34, f32[3,32,128]{2,1,0:T(8,128)S(1)} %constant_dynamic-slice_fusion.31, ...), kind=kLoop, calls=%fused_computation.36.clone.1 | loop fusion | flops 9412608 | bytes 2392064 | tf_op jit(solution)/shard_map/while/body/eval_jaxpr/reduce_sum | solution.py:61
  455.0 6.2 %fusion.161 = (f32[32,128,128]{2,1,0:T(8,128)}, f32[32,128,128]{2,1,0:T(8,128)}) fusion(f32[3,32,128]{2,1,0:T(8,128)S(1)} %constant_dynamic-slice_fusion.31, f32[3,32,128]{2,1,0:T(8,128)S(1)} %constant_dynamic-slice_fusion.32, f32[3,32,128]{2,1,0:T(8,128)S(1)} %constant_dynamic-slice_fusion.33, f32[3,32,128]{2,1,0:T(8,128)S(1)} %constant_dynamic-slice_fusion.34), kind=kLoop, calls=%fused_computation.32.clone.1 | loop fusion | flops 9961472 | bytes 4390912 | tf_op jit(solution)/shard_map/while/body/eval_jaxpr/reduce_sum | solution.py:46
  464.1 5.1 fusion.162
  470.4 6.0 %fusion.163 = (f32[3,32,128]{2,1,0:T(8,128)S(1)}, f32[3,32,128]{2,1,0:T(8,128)S(1)}) fusion(f32[32,128,128]{2,1,0:T(8,128)S(1)} %copy.207, f32[3,32,128]{2,1,0:T(8,128)S(1)} %constant_dynamic-slice_fusion.33, f32[3,32,128]{2,1,0:T(8,128)S(1)} %constant_dynamic-slice_fusion.34, f32[3,32,128]{2,1,0:T(8,128)S(1)} %constant_dynamic-slice_fusion.31, ...), kind=kLoop, calls=%fused_computation.36.clone.1 | loop fusion | flops 9412608 | bytes 2392064 | tf_op jit(solution)/shard_map/while/body/eval_jaxpr/reduce_sum | solution.py:61
  479.6 6.2 %fusion.161 = (f32[32,128,128]{2,1,0:T(8,128)}, f32[32,128,128]{2,1,0:T(8,128)}) fusion(f32[3,32,128]{2,1,0:T(8,128)S(1)} %constant_dynamic-slice_fusion.31, f32[3,32,128]{2,1,0:T(8,128)S(1)} %constant_dynamic-slice_fusion.32, f32[3,32,128]{2,1,0:T(8,128)S(1)} %constant_dynamic-slice_fusion.33, f32[3,32,128]{2,1,0:T(8,128)S(1)} %constant_dynamic-slice_fusion.34), kind=kLoop, calls=%fused_computation.32.clone.1 | loop fusion | flops 9961472 | bytes 4390912 | tf_op jit(solution)/shard_map/while/body/eval_jaxpr/reduce_sum | solution.py:46
  488.7 5.1 fusion.162
  495.0 6.0 %fusion.163 = (f32[3,32,128]{2,1,0:T(8,128)S(1)}, f32[3,32,128]{2,1,0:T(8,128)S(1)}) fusion(f32[32,128,128]{2,1,0:T(8,128)S(1)} %copy.207, f32[3,32,128]{2,1,0:T(8,128)S(1)} %constant_dynamic-slice_fusion.33, f32[3,32,128]{2,1,0:T(8,128)S(1)} %constant_dynamic-slice_fusion.34, f32[3,32,128]{2,1,0:T(8,128)S(1)} %constant_dynamic-slice_fusion.31, ...), kind=kLoop, calls=%fused_computation.36.clone.1 | loop fusion | flops 9412608 | bytes 2392064 | tf_op jit(solution)/shard_map/while/body/eval_jaxpr/reduce_sum | solution.py:61
  503.3 3.7 all-to-all-start.3
  508.4 4.5 collective-permute-start.9
  513.0 3.8 collective-permute-done.8
  516.9 3.2 collective-permute-start.10
  522.0 3.9 collective-permute-done.11
  (523 shorter events, 149.0 us)
Async XLA Ops:
  6.5 14.2 %copy-start.16 = (f32[64,128]{1,0:T(8,128)S(1)}, f32[64,128]{1,0:T(8,128)}, u32[]{:S(2)}) copy-start(f32[64,128]{1,0:T(8,128)} %param.17) | copy-start | bytes 98308
  6.5 20.7 %copy-start.37 = (s32[256,2]{0,1:T(2,128)S(1)}, s32[256,2]{0,1:T(2,128)}, u32[]{:S(2)}) copy-start(s32[256,2]{0,1:T(2,128)} %param.21) | copy-start | bytes 6148
  6.5 35.1 %all-to-all-start = ((f32[7,16,32,128]{3,2,0,1:T(8,128)}), f32[7,16,32,128]{3,2,0,1:T(8,128)S(1)}, u32[]{:S(2)}, u32[]{:S(2)}) async-start(f32[7,16,32,128]{3,2,0,1:T(8,128)} %copy.103), calls=%async_computation | async-start | bytes 3670016 | tf_op jit(solution)/shard_map/all_to_all | solution.py:113
  14.2 234.9 %collective-permute-start = (f32[2,1,128]{2,1,0:T(1,128)}, f32[2,1,128]{2,1,0:T(1,128)}, u32[]{:S(2)}, u32[]{:S(2)}) collective-permute-start(f32[2,1,128]{2,1,0:T(1,128)} %get-tuple-element.382), channel_id=1, source_target_pairs={{8,0},{16,8},{24,16},{32,24},{40,32},{48,40},{56,48},{64,56},{72,6... | collective-permute-start | bytes 3080 | tf_op jit(solution)/shard_map/ppermute | solution.py:29
  15.5 233.6 %collective-permute-start.2 = (f32[2,1,128]{2,1,0:T(1,128)}, f32[2,1,128]{2,1,0:T(1,128)}, u32[]{:S(2)}, u32[]{:S(2)}) collective-permute-start(f32[2,1,128]{2,1,0:T(1,128)} %get-tuple-element.381), channel_id=1, source_target_pairs={{0,8},{8,16},{16,24},{24,32},{32,40},{40,48},{48,56},{56,64},{64,7... | collective-permute-start | bytes 3080 | tf_op jit(solution)/shard_map/ppermute | solution.py:27
  20.7 17.2 %collective-permute-start.1 = (f32[1,128]{1,0:T(1,128)S(1)}, f32[1,128]{1,0:T(1,128)S(1)}, u32[]{:S(2)}, u32[]{:S(2)}) collective-permute-start(f32[1,128]{1,0:T(1,128)S(1)} %get-tuple-element.392), channel_id=1, source_target_pairs={{8,0},{16,8},{24,16},{32,24},{40,32},{48,40},{56,48},{64,56},{72,6... | collective-permute-start | bytes 1544 | tf_op jit(solution)/shard_map/ppermute | solution.py:29
  22.0 15.9 %collective-permute-start.3 = (f32[1,128]{1,0:T(1,128)S(1)}, f32[1,128]{1,0:T(1,128)S(1)}, u32[]{:S(2)}, u32[]{:S(2)}) collective-permute-start(f32[1,128]{1,0:T(1,128)S(1)} %get-tuple-element.391), channel_id=1, source_target_pairs={{0,8},{8,16},{16,24},{24,32},{32,40},{40,48},{48,56},{56,64},{64,7... | collective-permute-start | bytes 1544 | tf_op jit(solution)/shard_map/ppermute | solution.py:27
  27.2 215.7 %copy-start.31 = (s32[256,1]{0,1:T(1,128)}, s32[256,1]{0,1:T(1,128)S(1)}, u32[]{:S(2)}) copy-start(s32[256,1]{0,1:T(1,128)S(1)} %get-tuple-element.393) | copy-start | bytes 3076
  27.2 216.3 %copy-start.29 = (s32[256,1]{0,1:T(1,128)}, s32[256,1]{0,1:T(1,128)S(1)}, u32[]{:S(2)}) copy-start(s32[256,1]{0,1:T(1,128)S(1)} %get-tuple-element.394) | copy-start | bytes 3076
  46.5 9.2 %copy-start.5 = (f32[3,256,128]{2,1,0:T(8,128)}, f32[3,256,128]{2,1,0:T(8,128)S(1)}, u32[]{:S(2)}) copy-start(f32[3,256,128]{2,1,0:T(8,128)S(1)} %get-tuple-element.578) | copy-start | bytes 1179652 | tf_op jit(solution)/shard_map/while
  46.5 9.2 %copy-start.7 = (f32[3,256,128]{2,1,0:T(8,128)}, f32[3,256,128]{2,1,0:T(8,128)S(1)}, u32[]{:S(2)}) copy-start(f32[3,256,128]{2,1,0:T(8,128)S(1)} %get-tuple-element.577) | copy-start | bytes 1179652 | tf_op jit(solution)/shard_map/while
  71.0 9.2 %copy-start.5 = (f32[3,256,128]{2,1,0:T(8,128)}, f32[3,256,128]{2,1,0:T(8,128)S(1)}, u32[]{:S(2)}) copy-start(f32[3,256,128]{2,1,0:T(8,128)S(1)} %get-tuple-element.578) | copy-start | bytes 1179652 | tf_op jit(solution)/shard_map/while
  71.0 9.2 %copy-start.7 = (f32[3,256,128]{2,1,0:T(8,128)}, f32[3,256,128]{2,1,0:T(8,128)S(1)}, u32[]{:S(2)}) copy-start(f32[3,256,128]{2,1,0:T(8,128)S(1)} %get-tuple-element.577) | copy-start | bytes 1179652 | tf_op jit(solution)/shard_map/while
  95.6 9.2 %copy-start.5 = (f32[3,256,128]{2,1,0:T(8,128)}, f32[3,256,128]{2,1,0:T(8,128)S(1)}, u32[]{:S(2)}) copy-start(f32[3,256,128]{2,1,0:T(8,128)S(1)} %get-tuple-element.578) | copy-start | bytes 1179652 | tf_op jit(solution)/shard_map/while
  95.6 9.2 %copy-start.7 = (f32[3,256,128]{2,1,0:T(8,128)}, f32[3,256,128]{2,1,0:T(8,128)S(1)}, u32[]{:S(2)}) copy-start(f32[3,256,128]{2,1,0:T(8,128)S(1)} %get-tuple-element.577) | copy-start | bytes 1179652 | tf_op jit(solution)/shard_map/while
  120.1 9.2 %copy-start.5 = (f32[3,256,128]{2,1,0:T(8,128)}, f32[3,256,128]{2,1,0:T(8,128)S(1)}, u32[]{:S(2)}) copy-start(f32[3,256,128]{2,1,0:T(8,128)S(1)} %get-tuple-element.578) | copy-start | bytes 1179652 | tf_op jit(solution)/shard_map/while
  144.7 9.2 %copy-start.5 = (f32[3,256,128]{2,1,0:T(8,128)}, f32[3,256,128]{2,1,0:T(8,128)S(1)}, u32[]{:S(2)}) copy-start(f32[3,256,128]{2,1,0:T(8,128)S(1)} %get-tuple-element.578) | copy-start | bytes 1179652 | tf_op jit(solution)/shard_map/while
  169.2 9.2 %copy-start.5 = (f32[3,256,128]{2,1,0:T(8,128)}, f32[3,256,128]{2,1,0:T(8,128)S(1)}, u32[]{:S(2)}) copy-start(f32[3,256,128]{2,1,0:T(8,128)S(1)} %get-tuple-element.578) | copy-start | bytes 1179652 | tf_op jit(solution)/shard_map/while
  193.8 9.2 %copy-start.5 = (f32[3,256,128]{2,1,0:T(8,128)}, f32[3,256,128]{2,1,0:T(8,128)S(1)}, u32[]{:S(2)}) copy-start(f32[3,256,128]{2,1,0:T(8,128)S(1)} %get-tuple-element.578) | copy-start | bytes 1179652 | tf_op jit(solution)/shard_map/while
  218.4 9.2 %copy-start.5 = (f32[3,256,128]{2,1,0:T(8,128)}, f32[3,256,128]{2,1,0:T(8,128)S(1)}, u32[]{:S(2)}) copy-start(f32[3,256,128]{2,1,0:T(8,128)S(1)} %get-tuple-element.578) | copy-start | bytes 1179652 | tf_op jit(solution)/shard_map/while
  244.2 18.6 %copy-start.17 = (f32[64,128]{1,0:T(8,128)S(1)}, f32[64,128]{1,0:T(8,128)}, u32[]{:S(2)}) copy-start(f32[64,128]{1,0:T(8,128)} %param.17) | copy-start | bytes 98308
  244.2 18.6 %copy-start.20 = (s32[64,128]{1,0:T(8,128)S(1)}, s32[64,128]{1,0:T(8,128)}, u32[]{:S(2)}) copy-start(s32[64,128]{1,0:T(8,128)} %param.19) | copy-start | bytes 98308
  244.2 18.6 %copy-start.21 = (f32[64,128]{1,0:T(8,128)S(1)}, f32[64,128]{1,0:T(8,128)}, u32[]{:S(2)}) copy-start(f32[64,128]{1,0:T(8,128)} %param.18) | copy-start | bytes 98308
  244.2 18.6 %copy-start.34 = (f32[1,128]{1,0:T(1,128)S(1)}, f32[1,128]{1,0:T(1,128)}, u32[]{:S(2)}) copy-start(f32[1,128]{1,0:T(1,128)} %copy-done.33) | copy-start | bytes 1540
  244.3 18.6 %copy-start.36 = (f32[1,128]{1,0:T(1,128)S(1)}, f32[1,128]{1,0:T(1,128)}, u32[]{:S(2)}) copy-start(f32[1,128]{1,0:T(1,128)} %copy-done.35) | copy-start | bytes 1540
  245.2 19.3 %copy-start.27 = (s32[512]{0:T(512)S(1)}, s32[512]{0:T(512)}, u32[]{:S(2)}) copy-start(s32[512]{0:T(512)} %copy-done.26) | copy-start | bytes 6148
  245.2 19.2 %all-to-all-start.1 = ((f32[3,16,32,128]{3,2,0,1:T(8,128)}), f32[3,16,32,128]{3,2,0,1:T(8,128)S(1)}, u32[]{:S(2)}, u32[]{:S(2)}) async-start(f32[3,16,32,128]{3,2,0,1:T(8,128)} %copy.113), calls=%async_computation.1 | async-start | bytes 1572864 | tf_op jit(solution)/shard_map/all_to_all | solution.py:152
  249.1 15.9 %copy-start = (f32[3,8192]{1,0:T(4,128)S(1)}, f32[3,8192]{1,0:T(4,128)}, u32[]{:S(2)}) copy-start(f32[3,8192]{1,0:T(4,128)} %param.15) | copy-start | bytes 294916
  249.1 15.9 %copy-start.13 = (f32[3,8192]{1,0:T(4,128)S(1)}, f32[3,8192]{1,0:T(4,128)}, u32[]{:S(2)}) copy-start(f32[3,8192]{1,0:T(4,128)} %param.16) | copy-start | bytes 294916
  249.2 16.0 %copy-start.10 = (f32[1,3,64,128]{3,2,1,0:T(8,128)S(1)}, f32[1,3,64,128]{3,2,1,0:T(8,128)}, u32[]{:S(2)}) copy-start(f32[1,3,64,128]{3,2,1,0:T(8,128)} %copy-done.9) | copy-start | bytes 294916
  250.0 12.8 %collective-permute-start.4 = (f32[2,66,1]{2,1,0:T(8,128)S(1)}, f32[2,66,1]{2,1,0:T(8,128)S(1)}, u32[]{:S(2)}, u32[]{:S(2)}) collective-permute-start(f32[2,66,1]{2,1,0:T(8,128)S(1)} %get-tuple-element.380), channel_id=1, source_target_pairs={{1,0},{2,1},{3,2},{4,3},{5,4},{6,5},{7,6},{9,8},{10,9},{11,10},{12... | collective-permute-start | bytes 1592 | tf_op jit(solution)/shard_map/ppermute | solution.py:29
  251.9 10.9 %collective-permute-start.6 = (f32[2,66,1]{2,1,0:T(8,128)S(1)}, f32[2,66,1]{2,1,0:T(8,128)S(1)}, u32[]{:S(2)}, u32[]{:S(2)}) collective-permute-start(f32[2,66,1]{2,1,0:T(8,128)S(1)} %get-tuple-element.379), channel_id=1, source_target_pairs={{0,1},{1,2},{2,3},{3,4},{4,5},{5,6},{6,7},{8,9},{9,10},{10,11},{11... | collective-permute-start | bytes 1592 | tf_op jit(solution)/shard_map/ppermute | solution.py:27
  254.3 5.3 collective-permute-start.5
  257.5 5.3 collective-permute-start.7
  267.5 31.8 %all-to-all-start.2 = ((f32[7,16,32,128]{3,2,0,1:T(8,128)}), f32[7,16,32,128]{3,2,0,1:T(8,128)S(1)}, u32[]{:S(2)}, u32[]{:S(2)}) async-start(f32[7,16,32,128]{3,2,0,1:T(8,128)} %copy.115), calls=%async_computation.2 | async-start | bytes 3670016 | tf_op jit(solution)/shard_map/all_to_all | solution.py:113
  274.7 24.8 %copy-start.32 = (s32[256,1]{0,1:T(1,128)S(1)}, s32[256,1]{0,1:T(1,128)}, u32[]{:S(2)}) copy-start(s32[256,1]{0,1:T(1,128)} %copy-done.31) | copy-start | bytes 3076
  304.2 9.3 %copy-start.1 = (f32[3,256,128]{2,1,0:T(8,128)}, f32[3,256,128]{2,1,0:T(8,128)S(1)}, u32[]{:S(2)}) copy-start(f32[3,256,128]{2,1,0:T(8,128)S(1)} %get-tuple-element.623) | copy-start | bytes 1179652 | tf_op jit(solution)/shard_map/while
  304.2 9.3 %copy-start.3 = (f32[3,256,128]{2,1,0:T(8,128)}, f32[3,256,128]{2,1,0:T(8,128)S(1)}, u32[]{:S(2)}) copy-start(f32[3,256,128]{2,1,0:T(8,128)S(1)} %get-tuple-element.622) | copy-start | bytes 1179652 | tf_op jit(solution)/shard_map/while
  328.8 9.3 %copy-start.1 = (f32[3,256,128]{2,1,0:T(8,128)}, f32[3,256,128]{2,1,0:T(8,128)S(1)}, u32[]{:S(2)}) copy-start(f32[3,256,128]{2,1,0:T(8,128)S(1)} %get-tuple-element.623) | copy-start | bytes 1179652 | tf_op jit(solution)/shard_map/while
  328.8 9.3 %copy-start.3 = (f32[3,256,128]{2,1,0:T(8,128)}, f32[3,256,128]{2,1,0:T(8,128)S(1)}, u32[]{:S(2)}) copy-start(f32[3,256,128]{2,1,0:T(8,128)S(1)} %get-tuple-element.622) | copy-start | bytes 1179652 | tf_op jit(solution)/shard_map/while
  353.4 9.3 %copy-start.1 = (f32[3,256,128]{2,1,0:T(8,128)}, f32[3,256,128]{2,1,0:T(8,128)S(1)}, u32[]{:S(2)}) copy-start(f32[3,256,128]{2,1,0:T(8,128)S(1)} %get-tuple-element.623) | copy-start | bytes 1179652 | tf_op jit(solution)/shard_map/while
  353.4 9.3 %copy-start.3 = (f32[3,256,128]{2,1,0:T(8,128)}, f32[3,256,128]{2,1,0:T(8,128)S(1)}, u32[]{:S(2)}) copy-start(f32[3,256,128]{2,1,0:T(8,128)S(1)} %get-tuple-element.622) | copy-start | bytes 1179652 | tf_op jit(solution)/shard_map/while
  378.0 9.3 %copy-start.1 = (f32[3,256,128]{2,1,0:T(8,128)}, f32[3,256,128]{2,1,0:T(8,128)S(1)}, u32[]{:S(2)}) copy-start(f32[3,256,128]{2,1,0:T(8,128)S(1)} %get-tuple-element.623) | copy-start | bytes 1179652 | tf_op jit(solution)/shard_map/while
  378.0 9.3 %copy-start.3 = (f32[3,256,128]{2,1,0:T(8,128)}, f32[3,256,128]{2,1,0:T(8,128)S(1)}, u32[]{:S(2)}) copy-start(f32[3,256,128]{2,1,0:T(8,128)S(1)} %get-tuple-element.622) | copy-start | bytes 1179652 | tf_op jit(solution)/shard_map/while
  402.6 9.3 %copy-start.1 = (f32[3,256,128]{2,1,0:T(8,128)}, f32[3,256,128]{2,1,0:T(8,128)S(1)}, u32[]{:S(2)}) copy-start(f32[3,256,128]{2,1,0:T(8,128)S(1)} %get-tuple-element.623) | copy-start | bytes 1179652 | tf_op jit(solution)/shard_map/while
  402.6 9.3 %copy-start.3 = (f32[3,256,128]{2,1,0:T(8,128)}, f32[3,256,128]{2,1,0:T(8,128)S(1)}, u32[]{:S(2)}) copy-start(f32[3,256,128]{2,1,0:T(8,128)S(1)} %get-tuple-element.622) | copy-start | bytes 1179652 | tf_op jit(solution)/shard_map/while
  427.3 9.3 %copy-start.1 = (f32[3,256,128]{2,1,0:T(8,128)}, f32[3,256,128]{2,1,0:T(8,128)S(1)}, u32[]{:S(2)}) copy-start(f32[3,256,128]{2,1,0:T(8,128)S(1)} %get-tuple-element.623) | copy-start | bytes 1179652 | tf_op jit(solution)/shard_map/while
  427.3 9.3 %copy-start.3 = (f32[3,256,128]{2,1,0:T(8,128)}, f32[3,256,128]{2,1,0:T(8,128)S(1)}, u32[]{:S(2)}) copy-start(f32[3,256,128]{2,1,0:T(8,128)S(1)} %get-tuple-element.622) | copy-start | bytes 1179652 | tf_op jit(solution)/shard_map/while
  451.9 9.3 %copy-start.1 = (f32[3,256,128]{2,1,0:T(8,128)}, f32[3,256,128]{2,1,0:T(8,128)S(1)}, u32[]{:S(2)}) copy-start(f32[3,256,128]{2,1,0:T(8,128)S(1)} %get-tuple-element.623) | copy-start | bytes 1179652 | tf_op jit(solution)/shard_map/while
  451.9 9.3 %copy-start.3 = (f32[3,256,128]{2,1,0:T(8,128)}, f32[3,256,128]{2,1,0:T(8,128)S(1)}, u32[]{:S(2)}) copy-start(f32[3,256,128]{2,1,0:T(8,128)S(1)} %get-tuple-element.622) | copy-start | bytes 1179652 | tf_op jit(solution)/shard_map/while
  476.5 9.3 %copy-start.1 = (f32[3,256,128]{2,1,0:T(8,128)}, f32[3,256,128]{2,1,0:T(8,128)S(1)}, u32[]{:S(2)}) copy-start(f32[3,256,128]{2,1,0:T(8,128)S(1)} %get-tuple-element.623) | copy-start | bytes 1179652 | tf_op jit(solution)/shard_map/while
  476.5 9.3 %copy-start.3 = (f32[3,256,128]{2,1,0:T(8,128)}, f32[3,256,128]{2,1,0:T(8,128)S(1)}, u32[]{:S(2)}) copy-start(f32[3,256,128]{2,1,0:T(8,128)S(1)} %get-tuple-element.622) | copy-start | bytes 1179652 | tf_op jit(solution)/shard_map/while
  502.4 23.5 %copy-start.22 = (f32[64,128]{1,0:T(8,128)S(1)}, f32[64,128]{1,0:T(8,128)}, u32[]{:S(2)}) copy-start(f32[64,128]{1,0:T(8,128)} %get-tuple-element.371) | copy-start | bytes 98308
  502.4 23.5 %copy-start.23 = (f32[64,128]{1,0:T(8,128)S(1)}, f32[64,128]{1,0:T(8,128)}, u32[]{:S(2)}) copy-start(f32[64,128]{1,0:T(8,128)} %get-tuple-element.372) | copy-start | bytes 98308
  502.4 23.5 %copy-start.24 = (f32[64,128]{1,0:T(8,128)S(1)}, f32[64,128]{1,0:T(8,128)}, u32[]{:S(2)}) copy-start(f32[64,128]{1,0:T(8,128)} %get-tuple-element.373) | copy-start | bytes 98308
  502.4 23.5 %copy-start.25 = (f32[64,128]{1,0:T(8,128)S(1)}, f32[64,128]{1,0:T(8,128)}, u32[]{:S(2)}) copy-start(f32[64,128]{1,0:T(8,128)} %get-tuple-element.374) | copy-start | bytes 98308
  503.3 23.4 %copy-start.28 = (s32[512]{0:T(512)S(1)}, s32[512]{0:T(512)}, u32[]{:S(2)}) copy-start(s32[512]{0:T(512)} %copy-done.26) | copy-start | bytes 6148
  503.3 23.8 %copy-start.12 = (f32[1,3,64,128]{3,2,1,0:T(8,128)S(1)}, f32[1,3,64,128]{3,2,1,0:T(8,128)}, u32[]{:S(2)}) copy-start(f32[1,3,64,128]{3,2,1,0:T(8,128)} %copy-done.11) | copy-start | bytes 294916
  503.3 23.8 %copy-start.14 = (f32[3,8192]{1,0:T(4,128)S(1)}, f32[3,8192]{1,0:T(4,128)}, u32[]{:S(2)}) copy-start(f32[3,8192]{1,0:T(4,128)} %param.16) | copy-start | bytes 294916
  503.3 23.3 %all-to-all-start.3 = ((f32[3,16,32,128]{3,2,0,1:T(8,128)}), f32[3,16,32,128]{3,2,0,1:T(8,128)S(1)}, u32[]{:S(2)}, u32[]{:S(2)}) async-start(f32[3,16,32,128]{3,2,0,1:T(8,128)} %copy.125), calls=%async_computation.3 | async-start | bytes 1572864 | tf_op jit(solution)/shard_map/all_to_all | solution.py:152
  507.1 9.7 %collective-permute-start.8 = (f32[1,128]{1,0:T(1,128)S(1)}, f32[1,128]{1,0:T(1,128)S(1)}, u32[]{:S(2)}, u32[]{:S(2)}) collective-permute-start(f32[1,128]{1,0:T(1,128)S(1)} %get-tuple-element.388), channel_id=1, source_target_pairs={{8,0},{16,8},{24,16},{32,24},{40,32},{48,40},{56,48},{64,56},{72,6... | collective-permute-start | bytes 1544 | tf_op jit(solution)/shard_map/ppermute | solution.py:29
  508.4 8.4 %collective-permute-start.9 = (f32[1,128]{1,0:T(1,128)S(1)}, f32[1,128]{1,0:T(1,128)S(1)}, u32[]{:S(2)}, u32[]{:S(2)}) collective-permute-start(f32[1,128]{1,0:T(1,128)S(1)} %get-tuple-element.387), channel_id=1, source_target_pairs={{0,8},{8,16},{16,24},{24,32},{32,40},{40,48},{48,56},{56,64},{64,7... | collective-permute-start | bytes 1544 | tf_op jit(solution)/shard_map/ppermute | solution.py:27
  516.9 5.1 collective-permute-start.10
  520.0 5.9 %collective-permute-start.11 = (f32[66,1]{1,0:T(8,128)S(1)}, f32[66,1]{1,0:T(8,128)S(1)}, u32[]{:S(2)}, u32[]{:S(2)}) collective-permute-start(f32[66,1]{1,0:T(8,128)S(1)} %get-tuple-element.384), channel_id=1, source_target_pairs={{0,1},{1,2},{2,3},{3,4},{4,5},{5,6},{6,7},{8,9},{9,10},{10,11},{11... | collective-permute-start | bytes 800 | tf_op jit(solution)/shard_map/ppermute | solution.py:27
  (48 other events, 281.5 us)
where the time goes:
time: 538 us; the launch traced here: 528 us
  other arithmetic  284 us (53%)
  local copies, waits for them, and re-layouts  112 us (21%)
  starting transfers between devices  54.7 us (10%)
  waiting for transfers between devices  49.2 us (9%)
  matrix products  14.1 us (3%)
  loops' own time  12.4 us (2%)
    reduce_sum x16, other arithmetic, tile_forces(): rest_sq = jnp.sum(offset * offset, axis=0)  98.6 us
    reduce_sum x16, other arithmetic, tile_forces(): return (jnp.sum(bond_force, axis=3), -jnp.sum(bond_force, axis=2))  96.5 us
    div x16, other arithmetic, tile_forces(): stiffness * flags * alive[:, None, None] * influence  81 us
    all_to_all x2, waiting for transfers between devices, body(): lax.all_to_all(chosen.reshape(outbound_field.shape[0], peers, capacity, w...  27.6 us
    ppermute x6, starting transfers between devices, extended(): lax.ppermute(tail, axis, [(i, (i + 1) % count) for i in range(ends)])  20.7 us
    div x16, local copies, waits for them, and re-layouts, tile_forces(): stiffness * flags * alive[:, None, None] * influence  19.5 us
    dynamic_slice x16, local copies, waits for them, and re-layouts, one_group(): packed = lax.dynamic_slice_in_dim(bond_flags, index * group, group, 0)  14.9 us
    ppermute x6, waiting for transfers between devices, extended(): lax.ppermute(head, axis, [((i + 1) % count, i) for i in range(ends)])  14.4 us
  transfers between devices with their start and end apart: 16, of which 6 were waited for; matrix products, arithmetic and copies ran while one was open for 38% of the time, Pallas kernels for 0%

commit v1 on v0

v1 whole, which is shorter than its diff:
```python
import functools

import jax
import jax.numpy as jnp
from jax import lax
from jax.experimental import pallas as pl
from jax.experimental.pallas import tpu as pltpu
from jax.sharding import PartitionSpec as P

MESH = pl.DeviceIdType.MESH
F32 = jnp.float32
BF16 = jnp.bfloat16

STEPS = 2
SOFT = 0.0025
REACH = 0.09
COUPLING = 0.3
DT = 0.2
FORCE_SCALE = 4.0 * REACH
FLOW = 1.0

NB = 64
CAP = 32
PAIRS = 256
SIDE = 4
PEERS = SIDE * SIDE
GROUP = 8
OFFSETS = [(dy, dx) for dy in range(SIDE) for dx in range(SIDE)]


def dot(a, b, ca=1, cb=0):
    return lax.dot_general(a, b, (((ca,), (cb,)), ((), ())), preferred_element_type=F32)


def split(t):
    high = t.astype(BF16)
    rest = t - high.astype(F32)
    mid = rest.astype(BF16)
    low = (rest - mid.astype(F32)).astype(BF16)
    return high, mid, low


def stack(parts):
    return jnp.concatenate(parts, axis=0)


def pair_rows(first, second, with_pressure):
    row = lax.broadcasted_iota(jnp.int32, (8, 128), 0)
    coord = row < 3
    centre = jnp.where(coord, jnp.broadcast_to(first[:, 0:1], (8, 128)), 0.0)
    a = first - centre
    b = second - centre
    norm_a = jnp.sum(jnp.where(coord, a * a, 0.0), axis=0, keepdims=True) + SOFT
    norm_b = jnp.sum(jnp.where(coord, b * b, 0.0), axis=0, keepdims=True)
    left = jnp.where(coord, a, jnp.where(row == 3, norm_a, jnp.where(row == 5, 1.0, 0.0)))
    right = jnp.where(coord, -2.0 * b, jnp.where(row == 3, 1.0, jnp.where(row == 5, norm_b, 0.0)))
    load = None
    if with_pressure:
        left = jnp.where(row == 4, first[3:4, :], left)
        load = jnp.where(row == 4, 1.0, jnp.where(row == 5, second[3:4, :], 0.0))
    return a, b, left, right, load


def six_left(parts):
    h, m, l = parts
    return stack([h, h, m, m, h, l])


def six_right(parts):
    h, m, l = parts
    return stack([h, m, h, m, l, h])


def tile_at(ref, slot):
    return ref[slot]


def rest_group(ks, pair_s, slots_ref, flags_ref, c1_ref, c2_ref):
    squares = []
    for k in ks:
        _, _, left, right, _ = pair_rows(
            tile_at(slots_ref, pair_s[0, k]), tile_at(slots_ref, pair_s[1, k]), False
        )
        squares.append((six_left(split(left)), six_right(split(right))))
    squares = [dot(left, right, 0, 0) for left, right in squares]
    sub = lax.broadcasted_iota(jnp.int32, (8, 128), 0)
    for k, square in zip(ks, squares):
        for t in range(16):
            w0, w1 = (8 * t) // 14, (8 * t + 7) // 14
            word = jnp.broadcast_to(flags_ref[w0, pl.ds(k, 1), :], (8, 128))
            if w1 != w0:
                other = jnp.broadcast_to(flags_ref[w1, pl.ds(k, 1), :], (8, 128))
                word = jnp.where(sub < (14 * w1 - 8 * t), word, other)
            bit = lax.shift_left(jnp.int32(1), lax.rem(sub + 8 * t, 14))
            value = jnp.maximum(square[8 * t : 8 * t + 8, :], SOFT)
            inverse = lax.rsqrt(value)
            q = lax.rsqrt(value + (REACH - SOFT))
            c2 = jnp.where(jnp.bitwise_and(word, bit) != 0, q * q, 0.0)
            c1_ref[k, pl.ds(8 * t, 8), :] = c2 * inverse
            c2_ref[k, pl.ds(8 * t, 8), :] = c2


def move_group(ks, pair_s, slots_ref, c1_ref, c2_ref, on_ref):
    pre = []
    for k in ks:
        a, b, left, right, load = pair_rows(
            tile_at(slots_ref, pair_s[0, k]), tile_at(slots_ref, pair_s[1, k]), True
        )
        ls, rs, ps = split(left), split(right), split(load)
        wide = jnp.concatenate([six_right(rs), six_right(ps)], axis=1)
        pre.append((a, b, six_left(ls), wide, stack(ls), stack(rs)))
    products = [dot(p[2], p[3], 0, 0) for p in pre]
    factors = []
    for k, product in zip(ks, products):
        highs, lows = [], []
        for t in range(8):
            rows = slice(16 * t, 16 * t + 16)
            square = jnp.maximum(product[rows, :128], SOFT)
            load = product[rows, 128:]
            f = c1_ref[k, pl.ds(16 * t, 16), :] - c2_ref[k, pl.ds(16 * t, 16), :] * (
                load * lax.rsqrt(square)
            )
            high = f.astype(BF16)
            highs.append(high)
            lows.append((f - high.astype(F32)).astype(BF16))
        factors.append((stack(highs), stack(lows)))
    sums = []
    for p, (high, low) in zip(pre, factors):
        sums.append(
            (dot(p[5], high, 1, 1) + dot(p[5], low, 1, 1), dot(p[4], high) + dot(p[4], low))
        )
    for k, p, (ga, gb) in zip(ks, pre, sums):
        ga = ga[0:8] + ga[8:16] + ga[16:24]
        gb = gb[0:8] + gb[8:16] + gb[16:24]
        on_a = -0.5 * ga - p[0] * ga[3:4, :]
        on_b = gb - p[1] * gb[5:6, :]
        on_ref[pl.ds(k, 3, stride=2 * PAIRS), :] = on_a[0:3]
        on_ref[pl.ds(PAIRS + k, 3, stride=2 * PAIRS), :] = on_b[0:3]


def kernel(
    pair_s, count_s, ref, disp, vel, pres, cond, mask, send_v, pair_v, flags_any,
    disp_o, vel_o, pres_o,
    flags, rest, shift, speed, owner, chooser, slots_rest, slots_move, on, c1, c2,
    ref_out, ref_in, mov_out0, mov_out1, mov_in0, mov_in1, frc_out0, frc_out1, frc_in0, frc_in1,
    cells0, cells1, west0, east0, west1, east1, north0, south0, north1, south1,
    face_n, face_s, face_w, face_e, press, wet,
    flag_sem, send_sem, recv_sem, halo_send, halo_recv,
):
    s = lax.axis_index("slab")
    u = lax.axis_index("sub")
    slabs = lax.axis_size("slab")
    subs = lax.axis_size("sub")
    y, x = s // SIDE, s % SIDE
    peer = {o: ((y + o[0]) % SIDE) * SIDE + (x + o[1]) % SIDE for o in OFFSETS}
    up, down = (s + slabs - 1) % slabs, (s + 1) % slabs
    left, right = (u + subs - 1) % subs, (u + 1) % subs

    barrier = pltpu.get_barrier_semaphore()
    for o in OFFSETS[1:]:
        pl.semaphore_signal(barrier, inc=1, device_id=(peer[o], u), device_id_type=MESH)
    for v in (left, right):
        pl.semaphore_signal(barrier, inc=1, device_id=(s, v), device_id_type=MESH)
    flag_copy = pltpu.make_async_copy(flags_any, flags, flag_sem)
    flag_copy.start()

    for l in range(NB):
        lanes = slice(128 * l, 128 * l + 128)
        r = ref[:, lanes]
        rest[pl.ds(l, 3, stride=NB), :] = r
        shift[pl.ds(l, 3, stride=NB), :] = disp[:, lanes]
        speed[pl.ds(l, 3, stride=NB), :] = vel[:, lanes]
    wet[...] = mask[...].astype(F32)
    press[...] = pres[...]
    slots_rest[...] = jnp.zeros_like(slots_rest)
    slots_move[...] = jnp.zeros_like(slots_move)
    chosen = jnp.concatenate([send_v[p : p + 1, :] for p in range(PEERS)], axis=1)
    block = lax.broadcasted_iota(jnp.int32, (NB, PEERS * CAP), 0)
    table = jnp.where(chosen == block, 1.0, 0.0)
    owner[...] = table.astype(BF16)
    chooser[...] = jnp.transpose(table).astype(BF16)

    def fields(buffer, count):
        return [buffer[f * NB : (f + 1) * NB, :] for f in range(count)]

    def placed():
        return [r + d for r, d in zip(fields(rest, 3), fields(shift, 3))]

    def remote(src, dst, phase, n, o):
        return pltpu.make_async_remote_copy(
            src_ref=src.at[peer[o]],
            dst_ref=dst.at[s],
            send_sem=send_sem.at[phase, n],
            recv_sem=recv_sem.at[phase, n],
            device_id=(peer[o], u),
            device_id_type=MESH,
        )

    def send_row(src, dst, phase, dy):
        copies = []
        for n, o in enumerate(OFFSETS):
            if o[0] == dy and o != (0, 0):
                copy = remote(src, dst, phase, n, o)
                copy.start()
                copies.append(copy)
        return copies

    def distribute(values, src, dst, phase):
        parts = split(jnp.concatenate(values, axis=1))
        copies = []
        for dy in (1, 2, 3, 0):
            row = (y + dy) % SIDE
            pick = chooser[pl.ds(pl.multiple_of(row * SIDE * CAP, SIDE * CAP), SIDE * CAP), :]
            picked = dot(pick, parts[0]) + dot(pick, parts[1]) + dot(pick, parts[2])
            for q in range(SIDE):
                for f in range(len(values)):
                    src[row * SIDE + q, pl.ds(f * CAP, CAP), :] = picked[
                        q * CAP : (q + 1) * CAP, f * 128 : (f + 1) * 128
                    ]
            copies += send_row(src, dst, phase, dy)
        dst[s] = src[s]
        return copies

    def spread(src, dst, count):
        @pl.loop(0, PEERS)
        def _(p):
            for g in range(CAP // 8):
                for f in range(count):
                    dst[pl.ds(p * CAP + 8 * g, 8), f, :] = src[p, pl.ds(f * CAP + 8 * g, 8), :]

    def halo(src, n, dev, dst):
        return pltpu.make_async_remote_copy(
            src_ref=src, dst_ref=dst, send_sem=halo_send.at[n], recv_sem=halo_recv.at[n],
            device_id=dev, device_id_type=MESH,
        )

    cells0[0] = pres[...]
    cells0[1] = wet[...]
    cells0[2] = cond[...] * wet[...]
    pl.semaphore_wait(barrier, PEERS - 1 + 2)

    rest_copies = distribute(fields(rest, 3), ref_out, ref_in, 0)

    def load_of(pressure):
        return 0.5 + (0.5 * COUPLING) * (pressure * wet[...])

    move_copies = distribute(placed() + [load_of(press[...])], mov_out0, mov_in0, 1)

    halos = [
        halo(cells0.at[:, pl.ds(56, 8)], 0, (down, u), north0),
        halo(cells0.at[:, pl.ds(0, 8)], 1, (up, u), south0),
        halo(cells0, 2, (s, right), west0),
        halo(cells0, 3, (s, left), east0),
    ]
    for copy in halos:
        copy.start()

    for copy in rest_copies:
        copy.wait_recv()
    spread(ref_in, slots_rest, 3)
    flag_copy.wait()

    @pl.loop(0, PAIRS // GROUP)
    def _(j):
        rest_group(
            [j * GROUP + d for d in range(GROUP)], pair_s, slots_rest, flags, c1, c2
        )

    for copy in move_copies:
        copy.wait_recv()

    rows = lax.broadcasted_iota(jnp.int32, (64, 128), 0)
    lanes = lax.broadcasted_iota(jnp.int32, (64, 128), 1)

    def neighbours(centre, north, south, west, east):
        return (
            jnp.where(rows == 0, north[7:8, :], pltpu.roll(centre, 1, 0)),
            jnp.where(rows == 63, south[0:1, :], pltpu.roll(centre, 63, 0)),
            jnp.where(lanes == 0, pltpu.roll(west, 1, 1), pltpu.roll(centre, 1, 1)),
            jnp.where(lanes == 127, pltpu.roll(east, 127, 1), pltpu.roll(centre, 127, 1)),
        )

    def faces():
        inside = (
            jnp.logical_or(rows > 0, s > 0),
            jnp.logical_or(rows < 63, s < slabs - 1),
            jnp.logical_or(lanes > 0, u > 0),
            jnp.logical_or(lanes < 127, u < subs - 1),
        )
        wets = neighbours(wet[...], north0[1], south0[1], west0[1], east0[1])
        rocks = neighbours(cells0[2], north0[2], south0[2], west0[2], east0[2])
        for face, ok, w, r in zip((face_n, face_s, face_w, face_e), inside, wets, rocks):
            value = 0.5 * (cond[...] * wet[...] * w + r * wet[...])
            face[...] = jnp.where(ok, value, 0.0)

    def flow(north, south, west, east):
        centre = press[...]
        total = jnp.zeros_like(centre)
        around = neighbours(centre, north, south, west, east)
        for face, value in zip((face_s, face_n, face_e, face_w), (1, 0, 3, 2)):
            total = total + face[...] * (around[value] - centre)
        press[...] = centre + FLOW * total

    def pair_forces(mov_in):
        spread(mov_in, slots_move, 4)

        @pl.loop(0, PAIRS // GROUP)
        def _(j):
            move_group([j * GROUP + d for d in range(GROUP)], pair_s, slots_move, c1, c2, on)

    live = lax.broadcasted_iota(jnp.int32, (2, PAIRS), 1) < count_s[0]
    named = jnp.where(live, pair_v[...], -1)
    ends = jnp.concatenate([named[0:1, :], named[1:2, :]], axis=1)

    def give_back(src, dst, phase):
        parts = split(
            jnp.concatenate([on[f * 2 * PAIRS : (f + 1) * 2 * PAIRS, :] for f in range(3)], axis=1)
        )
        copies = []
        for dy in (1, 2, 3, 0):
            row = (y + dy) % SIDE
            slot = lax.broadcasted_iota(jnp.int32, (SIDE * CAP, 2 * PAIRS), 0) + row * (SIDE * CAP)
            hit = jnp.where(slot == ends, 1.0, 0.0).astype(BF16)
            total = dot(hit, parts[0]) + dot(hit, parts[1]) + dot(hit, parts[2])
            for q in range(SIDE):
                for f in range(3):
                    src[row * SIDE + q, pl.ds(f * CAP, CAP), :] = total[
                        q * CAP : (q + 1) * CAP, f * 128 : (f + 1) * 128
                    ]
            copies += send_row(src, dst, phase, dy)
        dst[s] = src[s]
        return copies

    def advance(frc_in):
        parts = split(
            jnp.concatenate(
                [
                    frc_in[:, f * CAP : (f + 1) * CAP, :].reshape(PEERS * CAP, 128)
                    for f in range(3)
                ],
                axis=1,
            )
        )
        table = owner[...]
        force = dot(table, parts[0]) + dot(table, parts[1]) + dot(table, parts[2])
        for f in range(3):
            part = slice(f * NB, (f + 1) * NB)
            v = speed[part, :] + (DT * FORCE_SCALE) * force[:, f * 128 : (f + 1) * 128]
            speed[part, :] = v
            shift[part, :] = shift[part, :] + DT * v

    pair_forces(mov_in0)
    back_copies = give_back(frc_out0, frc_in0, 2)
    for copy in halos:
        copy.wait_recv()
    faces()
    flow(north0[0], south0[0], west0[0], east0[0])
    cells1[...] = press[...]
    halos1 = [
        halo(cells1.at[pl.ds(56, 8)], 4, (down, u), north1),
        halo(cells1.at[pl.ds(0, 8)], 5, (up, u), south1),
        halo(cells1, 6, (s, right), west1),
        halo(cells1, 7, (s, left), east1),
    ]
    for copy in halos1:
        copy.start()
    for copy in back_copies:
        copy.wait_recv()
    advance(frc_in0)

    next_copies = distribute(placed() + [load_of(press[...])], mov_out1, mov_in1, 3)
    for copy in halos1:
        copy.wait_recv()
    flow(north1[...], south1[...], west1[...], east1[...])
    pres_o[...] = press[...]
    for copy in next_copies:
        copy.wait_recv()
    pair_forces(mov_in1)
    last_copies = give_back(frc_out1, frc_in1, 4)
    for copy in last_copies:
        copy.wait_recv()
    advance(frc_in1)
    for l in range(NB):
        lanes_l = slice(128 * l, 128 * l + 128)
        disp_o[:, lanes_l] = shift[pl.ds(l, 3, stride=NB), :]
        vel_o[:, lanes_l] = speed[pl.ds(l, 3, stride=NB), :]
    for copies in (rest_copies, move_copies, halos, back_copies, halos1, next_copies, last_copies):
        for copy in copies:
            copy.wait_send()


def body(ref_pos, disp, vel, pressure, conductivity, frac_mask, send_list, pair_list, pair_count, bond_flags):
    vmem = pl.BlockSpec(memory_space=pltpu.VMEM)
    smem = pl.BlockSpec(memory_space=pltpu.SMEM)
    pairs = pair_list.T
    grid = pltpu.VMEM((64, 128), F32)
    three = pltpu.VMEM((3 * NB, 128), F32)
    third = pltpu.VMEM((PEERS, 3 * CAP, 128), F32)
    fourth = pltpu.VMEM((PEERS, 4 * CAP, 128), F32)
    slots = pltpu.VMEM((PEERS * CAP, 8, 128), F32)
    grids = pltpu.VMEM((3, 64, 128), F32)
    strips = pltpu.VMEM((3, 8, 128), F32)
    strip = pltpu.VMEM((8, 128), F32)
    tiles = pltpu.VMEM((PAIRS, 128, 128), F32)
    return pl.pallas_call(
        kernel,
        out_shape=(
            jax.ShapeDtypeStruct(disp.shape, F32),
            jax.ShapeDtypeStruct(vel.shape, F32),
            jax.ShapeDtypeStruct(pressure.shape, F32),
        ),
        in_specs=[smem, smem] + [vmem] * 8 + [pl.BlockSpec(memory_space=pl.ANY)],
        out_specs=(vmem, vmem, vmem),
        scratch_shapes=[
            pltpu.VMEM((10, PAIRS, 128), jnp.int32),
            three, three, three,
            pltpu.VMEM((NB, PEERS * CAP), BF16),
            pltpu.VMEM((PEERS * CAP, NB), BF16),
            slots, slots,
            pltpu.VMEM((3 * 2 * PAIRS, 128), F32),
            tiles, tiles,
            third, third, fourth, fourth, fourth, fourth, third, third, third, third,
            grids, grid, grids, grids, grid, grid, strips, strips, strip, strip,
            grid, grid, grid, grid, grid, grid,
            pltpu.SemaphoreType.DMA,
            pltpu.SemaphoreType.DMA((5, PEERS)),
            pltpu.SemaphoreType.DMA((5, PEERS)),
            pltpu.SemaphoreType.DMA((8,)),
            pltpu.SemaphoreType.DMA((8,)),
        ],
        compiler_params=pltpu.CompilerParams(
            collective_id=0, has_side_effects=True, vmem_limit_bytes=58 << 20
        ),
    )(
        pairs, pair_count, ref_pos, disp, vel, pressure, conductivity, frac_mask, send_list, pairs,
        bond_flags.transpose(1, 0, 2),
    )


def solution(mesh):
    in_specs = (
        P(None, ("slab", "sub")),
        P(None, ("slab", "sub")),
        P(None, ("slab", "sub")),
        P("slab", "sub"),
        P("slab", "sub"),
        P("slab", "sub"),
        P(("slab", "sub"), None),
        P(("slab", "sub"), None),
        P(("slab", "sub")),
        P(("slab", "sub"), None, None),
    )
    out_specs = (P(None, ("slab", "sub")), P(None, ("slab", "sub")), P("slab", "sub"))
    return jax.shard_map(body, mesh=mesh, in_specs=in_specs, out_specs=out_specs, check_vma=False)
```

time: 538 us -> 140 us (0.26); the launches traced: 528 us -> 140 us
  other arithmetic: 284 us -> 0 us
  Pallas kernels: 0 us -> 134 us
  local copies, waits for them, and re-layouts: 112 us -> 4.54 us
  starting transfers between devices: 54.7 us -> 0 us
  waiting for transfers between devices: 49.2 us -> 0 us
  matrix products: 14.1 us -> 0 us
  loops' own time: 12.4 us -> 0 us
    reduce_sum x32 -> x0, other arithmetic: 195 us -> none  [the longest x16 98.6 us: tile_forces(): rest_sq = jnp.sum(offset * offset, axis=0)]
    pallas_call x0 -> x1, Pallas kernels: none -> 134 us  [body(): pl.pallas_call(kernel, out_shape=(jax.ShapeDtypeStruct(disp.shape, F32),...]
    div x16 -> x0, other arithmetic: 81 us -> none  [tile_forces(): stiffness * flags * alive[:, None, None] * influence]
    slice x78 -> x0, local copies, waits for them, and re-layouts: 38.2 us -> none  [the longest x16 13 us: tile_forces(): moving_first[:3, :, :, None]]
    ppermute x12 -> x0, starting transfers between devices: 32.7 us -> none  [the longest x6 20.7 us: extended(): lax.ppermute(tail, axis, [(i, (i + 1) % count) for i in range(ends)])]
    all_to_all x4 -> x0, waiting for transfers between devices: 27.7 us -> none  [the longest x2 27.6 us: body(): lax.all_to_all(chosen.reshape(outbound_field.shape[0], peers, capacity, w...]
    dynamic_slice x64 -> x0, local copies, waits for them, and re-layouts: 27.2 us -> none  [the longest x16 14.9 us: one_group(): packed = lax.dynamic_slice_in_dim(bond_flags, index * group, group, 0)]
    all_to_all x4 -> x0, starting transfers between devices: 22 us -> none  [the longest x2 14.4 us: body(): lax.all_to_all(chosen.reshape(outbound_field.shape[0], peers, capacity, w...]
  transfers between devices with their start and end apart: 16 -> 0, of which waited for: 6 -> 0; matrix products, arithmetic and copies ran while one was open for 38% -> 0% of each run, Pallas kernels for 0% -> 0%
where the time goes in v1:
time: 140 us
  Pallas kernels  134 us (96%)
  local copies, waits for them, and re-layouts  4.54 us (3%)
    pallas_call x1, Pallas kernels, body(): pl.pallas_call(kernel, out_shape=(jax.ShapeDtypeStruct(disp.shape, F32),...  134 us
    unnamed x3, local copies, waits for them, and re-layouts  4.54 us

profile of v1, /device:TPU:96, one launch (start us, length us, event | category | flops | bytes accessed | tf_op | source)
XLA Modules:
  0.0 140.2 jit_solution(14575255745084166334)
XLA Ops:
  1.3 134.4 %shard_map.121 = (f32[3,8192]{1,0:T(4,128)}, f32[3,8192]{1,0:T(4,128)}, f32[64,128]{1,0:T(8,128)}) custom-call(s32[2,256]{1,0:T(2,128)} %bitcast.3, s32[1]{0:T(128)S(6)} %copy.16.count_s, f32[3,8192]{1,0:T(4,128)} %ref.1, f32[3,8192]{1,0:T(4,128)} %disp.1, f32[3,8192]{1,0:T(4,128)} %vel.1, f32[64,128]{1,0:T(8,128)} %pres.1, f32[64,128]{1,0:T(8,128)} %cond.1, ...), custom_call_target="tpu_custom_call" | custom-call | tf_op jit(solution)/shard_map/pallas_call | solution.py:405
  135.7 1.6 %copy.17 = f32[3,8192]{1,0:T(4,128)} copy(f32[3,8192]{1,0:T(4,128)} %get-tuple-element.6) | data formatting | bytes 196608
  137.2 1.6 %copy.18 = f32[3,8192]{1,0:T(4,128)} copy(f32[3,8192]{1,0:T(4,128)} %get-tuple-element.7) | data formatting | bytes 196608
  138.8 1.4 copy.19

commit v2 on v1

--- a/solution.py
+++ b/solution.py
@@ -25,6 +25,7 @@
 SIDE = 4
 PEERS = SIDE * SIDE
 GROUP = 8
+REST_GROUP = 16
 OFFSETS = [(dy, dx) for dy in range(SIDE) for dx in range(SIDE)]
 
 
@@ -100,19 +101,20 @@
             c2_ref[k, pl.ds(8 * t, 8), :] = c2
 
 
-def move_group(ks, pair_s, slots_ref, c1_ref, c2_ref, on_ref):
+def bond_factors(buffer, ks, pair_s, slots_ref, c1_ref, c2_ref, factor, coords, tiles):
     pre = []
-    for k in ks:
+    for d, k in enumerate(ks):
         a, b, left, right, load = pair_rows(
             tile_at(slots_ref, pair_s[0, k]), tile_at(slots_ref, pair_s[1, k]), True
         )
         ls, rs, ps = split(left), split(right), split(load)
-        wide = jnp.concatenate([six_right(rs), six_right(ps)], axis=1)
-        pre.append((a, b, six_left(ls), wide, stack(ls), stack(rs)))
-    products = [dot(p[2], p[3], 0, 0) for p in pre]
-    factors = []
-    for k, product in zip(ks, products):
-        highs, lows = [], []
+        pre.append((six_left(ls), jnp.concatenate([six_right(rs), six_right(ps)], axis=1)))
+        coords[buffer, d, 0] = stack(ls[:2])
+        coords[buffer, d, 1] = stack(rs[:2])
+        tiles[buffer, d, 0] = a
+        tiles[buffer, d, 1] = b
+    products = [dot(left, right, 0, 0) for left, right in pre]
+    for d, (k, product) in enumerate(zip(ks, products)):
         for t in range(8):
             rows = slice(16 * t, 16 * t + 16)
             square = jnp.maximum(product[rows, :128], SOFT)
@@ -121,27 +123,38 @@
                 load * lax.rsqrt(square)
             )
             high = f.astype(BF16)
-            highs.append(high)
-            lows.append((f - high.astype(F32)).astype(BF16))
-        factors.append((stack(highs), stack(lows)))
+            factor[buffer, d, 0, rows, :] = high
+            factor[buffer, d, 1, rows, :] = (f - high.astype(F32)).astype(BF16)
+
+
+def bond_sums(buffer, ks, on_ref, factor, coords, tiles):
     sums = []
-    for p, (high, low) in zip(pre, factors):
+    for d in range(len(ks)):
+        ca, cb = coords[buffer, d, 0], coords[buffer, d, 1]
+        high, low = factor[buffer, d, 0], factor[buffer, d, 1]
         sums.append(
-            (dot(p[5], high, 1, 1) + dot(p[5], low, 1, 1), dot(p[4], high) + dot(p[4], low))
-        )
-    for k, p, (ga, gb) in zip(ks, pre, sums):
-        ga = ga[0:8] + ga[8:16] + ga[16:24]
-        gb = gb[0:8] + gb[8:16] + gb[16:24]
-        on_a = -0.5 * ga - p[0] * ga[3:4, :]
-        on_b = gb - p[1] * gb[5:6, :]
+            (
+                dot(
+                    jnp.concatenate([cb, cb], axis=1),
+                    jnp.concatenate([high, low], axis=1), 1, 1,
+                ),
+                dot(jnp.concatenate([ca, ca], axis=1), stack([high, low])),
+            )
+        )
+    for d, (k, (ga, gb)) in enumerate(zip(ks, sums)):
+        ga = ga[0:8] + ga[8:16]
+        gb = gb[0:8] + gb[8:16]
+        on_a = -0.5 * ga - tiles[buffer, d, 0] * ga[3:4, :]
+        on_b = gb - tiles[buffer, d, 1] * gb[5:6, :]
         on_ref[pl.ds(k, 3, stride=2 * PAIRS), :] = on_a[0:3]
         on_ref[pl.ds(PAIRS + k, 3, stride=2 * PAIRS), :] = on_b[0:3]
 
 
 def kernel(
     pair_s, count_s, ref, disp, vel, pres, cond, mask, send_v, pair_v, flags_any,
-    disp_o, vel_o, pres_o,
+    state,
     flags, rest, shift, speed, owner, chooser, slots_rest, slots_move, on, c1, c2,
+    factor, coords, tiles,
     ref_out, ref_in, mov_out0, mov_out1, mov_in0, mov_in1, frc_out0, frc_out1, frc_in0, frc_in1,
     cells0, cells1, west0, east0, west1, east1, north0, south0, north1, south1,
     face_n, face_s, face_w, face_e, press, wet,
@@ -260,10 +273,10 @@
     spread(ref_in, slots_rest, 3)
     flag_copy.wait()
 
-    @pl.loop(0, PAIRS // GROUP)
+    @pl.loop(0, PAIRS // REST_GROUP)
     def _(j):
         rest_group(
-            [j * GROUP + d for d in range(GROUP)], pair_s, slots_rest, flags, c1, c2
+            [j * REST_GROUP + d for d in range(REST_GROUP)], pair_s, slots_rest, flags, c1, c2
         )
 
     for copy in move_copies:
@@ -304,9 +317,28 @@
     def pair_forces(mov_in):
         spread(mov_in, slots_move, 4)
 
-        @pl.loop(0, PAIRS // GROUP)
-        def _(j):
-            move_group([j * GROUP + d for d in range(GROUP)], pair_s, slots_move, c1, c2, on)
+        def members(j):
+            return [j * GROUP + d for d in range(GROUP)]
+
+        def make(buffer, j):
+            bond_factors(buffer, members(j), pair_s, slots_move, c1, c2, factor, coords, tiles)
+
+        def add(buffer, j):
+            bond_sums(buffer, members(j), on, factor, coords, tiles)
+
+        groups = PAIRS // GROUP
+        make(0, 0)
+
+        @pl.loop(0, groups // 2 - 1)
+        def _(i):
+            add(0, 2 * i)
+            make(1, 2 * i + 1)
+            add(1, 2 * i + 1)
+            make(0, 2 * i + 2)
+
+        add(0, groups - 2)
+        make(1, groups - 1)
+        add(1, groups - 1)
 
     live = lax.broadcasted_iota(jnp.int32, (2, PAIRS), 1) < count_s[0]
     named = jnp.where(live, pair_v[...], -1)
@@ -372,7 +404,6 @@
     for copy in halos1:
         copy.wait_recv()
     flow(north1[...], south1[...], west1[...], east1[...])
-    pres_o[...] = press[...]
     for copy in next_copies:
         copy.wait_recv()
     pair_forces(mov_in1)
@@ -380,13 +411,20 @@
     for copy in last_copies:
         copy.wait_recv()
     advance(frc_in1)
-    for l in range(NB):
-        lanes_l = slice(128 * l, 128 * l + 128)
-        disp_o[:, lanes_l] = shift[pl.ds(l, 3, stride=NB), :]
-        vel_o[:, lanes_l] = speed[pl.ds(l, 3, stride=NB), :]
+    state[0 : 3 * NB, :] = shift[...]
+    state[3 * NB : 6 * NB, :] = speed[...]
+    state[6 * NB :, :] = press[...]
     for copies in (rest_copies, move_copies, halos, back_copies, halos1, next_copies, last_copies):
         for copy in copies:
             copy.wait_send()
+
+
+def unpack_kernel(state, disp_o, vel_o, pres_o):
+    for l in range(NB):
+        lanes = slice(128 * l, 128 * l + 128)
+        disp_o[:, lanes] = state[pl.ds(l, 3, stride=NB), :]
+        vel_o[:, lanes] = state[pl.ds(3 * NB + l, 3, stride=NB), :]
+    pres_o[...] = state[6 * NB :, :]
 
 
 def body(ref_pos, disp, vel, pressure, conductivity, frac_mask, send_list, pair_list, pair_count, bond_flags):
@@ -401,16 +439,12 @@
     grids = pltpu.VMEM((3, 64, 128), F32)
     strips = pltpu.VMEM((3, 8, 128), F32)
     strip = pltpu.VMEM((8, 128), F32)
-    tiles = pltpu.VMEM((PAIRS, 128, 128), F32)
-    return pl.pallas_call(
+    bonds = pltpu.VMEM((PAIRS, 128, 128), F32)
+    state = pl.pallas_call(
         kernel,
-        out_shape=(
-            jax.ShapeDtypeStruct(disp.shape, F32),
-            jax.ShapeDtypeStruct(vel.shape, F32),
-            jax.ShapeDtypeStruct(pressure.shape, F32),
-        ),
+        out_shape=jax.ShapeDtypeStruct((7 * NB, 128), F32),
         in_specs=[smem, smem] + [vmem] * 8 + [pl.BlockSpec(memory_space=pl.ANY)],
-        out_specs=(vmem, vmem, vmem),
+        out_specs=vmem,
         scratch_shapes=[
             pltpu.VMEM((10, PAIRS, 128), jnp.int32),
             three, three, three,
@@ -418,7 +452,10 @@
             pltpu.VMEM((PEERS * CAP, NB), BF16),
             slots, slots,
             pltpu.VMEM((3 * 2 * PAIRS, 128), F32),
-            tiles, tiles,
+            bonds, bonds,
+            pltpu.VMEM((2, GROUP, 2, 128, 128), BF16),
+            pltpu.VMEM((2, GROUP, 2, 16, 128), BF16),
+            pltpu.VMEM((2, GROUP, 2, 8, 128), F32),
             third, third, fourth, fourth, fourth, fourth, third, third, third, third,
             grids, grid, grids, grids, grid, grid, strips, strips, strip, strip,
             grid, grid, grid, grid, grid, grid,
@@ -435,6 +472,16 @@
         pairs, pair_count, ref_pos, disp, vel, pressure, conductivity, frac_mask, send_list, pairs,
         bond_flags.transpose(1, 0, 2),
     )
+    return pl.pallas_call(
+        unpack_kernel,
+        out_shape=(
+            jax.ShapeDtypeStruct(disp.shape, F32),
+            jax.ShapeDtypeStruct(vel.shape, F32),
+            jax.ShapeDtypeStruct(pressure.shape, F32),
+        ),
+        in_specs=[vmem],
+        out_specs=(vmem, vmem, vmem),
+    )(state)
 
 
 def solution(mesh):

time: 140 us -> 108 us (0.77)
  Pallas kernels: 134 us -> 106 us
  local copies, waits for them, and re-layouts: 4.54 us -> 0 us
    pallas_call x1 -> x2, Pallas kernels: 134 us -> 106 us  [the longest x1 104 us: body(): pl.pallas_call(kernel, out_shape=jax.ShapeDtypeStruct((7 * NB, 128), F32)...]
    unnamed x3 -> x0, local copies, waits for them, and re-layouts: 4.54 us -> none
where the time goes in v2:
time: 108 us
  Pallas kernels  106 us (98%)
  between operations  1.29 us (1%)
    pallas_call x1, Pallas kernels, body(): pl.pallas_call(kernel, out_shape=jax.ShapeDtypeStruct((7 * NB, 128), F32)...  104 us

profile of v2, /device:TPU:96, one launch (start us, length us, event | category | flops | bytes accessed | tf_op | source)
XLA Modules:
  0.0 107.5 jit_solution(17045793309158941997)
XLA Ops:
  1.3 104.5 %shard_map.121.state = f32[448,128]{1,0:T(8,128)} custom-call(s32[2,256]{1,0:T(2,128)} %bitcast.3, s32[1]{0:T(128)S(6)} %copy.13.count_s, f32[3,8192]{1,0:T(4,128)} %ref.1, f32[3,8192]{1,0:T(4,128)} %disp.1, f32[3,8192]{1,0:T(4,128)} %vel.1, f32[64,128]{1,0:T(8,128)} %pres.1, f32[64,128]{1,0:T(8,128)} %cond.1, s32[64,128]{1,0:T(8,128)} %mask.1, ...), custom_call_target="tpu_custom_call" | custom-call | tf_op jit(solution)/shard_map/pallas_call | solution.py:443
  105.7 1.8 %shard_map.122 = (f32[3,8192]{1,0:T(4,128)}, f32[3,8192]{1,0:T(4,128)}, f32[64,128]{1,0:T(8,128)}) custom-call(f32[448,128]{1,0:T(8,128)} %shard_map.121.state), custom_call_target="tpu_custom_call" | custom-call | tf_op jit(solution)/shard_map/pallas_call | solution.py:475

commit v3 on v2

--- a/solution.py
+++ b/solution.py
@@ -26,7 +26,10 @@
 PEERS = SIDE * SIDE
 GROUP = 8
 REST_GROUP = 16
-OFFSETS = [(dy, dx) for dy in range(SIDE) for dx in range(SIDE)]
+ORDER = [
+    (0, 1), (1, 0), (0, 3), (3, 0), (1, 1), (3, 3), (1, 3), (3, 1),
+    (0, 2), (2, 0), (1, 2), (2, 1), (3, 2), (2, 3), (2, 2),
+]
 
 
 def dot(a, b, ca=1, cb=0):
@@ -156,6 +159,7 @@
     flags, rest, shift, speed, owner, chooser, slots_rest, slots_move, on, c1, c2,
     factor, coords, tiles,
     ref_out, ref_in, mov_out0, mov_out1, mov_in0, mov_in1, frc_out0, frc_out1, frc_in0, frc_in1,
+    load_out, load_in,
     cells0, cells1, west0, east0, west1, east1, north0, south0, north1, south1,
     face_n, face_s, face_w, face_e, press, wet,
     flag_sem, send_sem, recv_sem, halo_send, halo_recv,
@@ -165,122 +169,82 @@
     slabs = lax.axis_size("slab")
     subs = lax.axis_size("sub")
     y, x = s // SIDE, s % SIDE
-    peer = {o: ((y + o[0]) % SIDE) * SIDE + (x + o[1]) % SIDE for o in OFFSETS}
+    odd = u % 2
+    targets, sources = [], []
+    for dy, dx in ORDER:
+        ty = dy + odd * ((SIDE - dx) % SIDE - dy)
+        tx = dx + odd * (dy - dx)
+        targets.append(((y + ty) % SIDE) * SIDE + (x + tx) % SIDE)
+        sources.append(((y + SIDE - ty) % SIDE) * SIDE + (x + SIDE - tx) % SIDE)
     up, down = (s + slabs - 1) % slabs, (s + 1) % slabs
     left, right = (u + subs - 1) % subs, (u + 1) % subs
 
     barrier = pltpu.get_barrier_semaphore()
-    for o in OFFSETS[1:]:
-        pl.semaphore_signal(barrier, inc=1, device_id=(peer[o], u), device_id_type=MESH)
+    for target in targets:
+        pl.semaphore_signal(barrier, inc=1, device_id=(target, u), device_id_type=MESH)
     for v in (left, right):
         pl.semaphore_signal(barrier, inc=1, device_id=(s, v), device_id_type=MESH)
     flag_copy = pltpu.make_async_copy(flags_any, flags, flag_sem)
     flag_copy.start()
 
-    for l in range(NB):
-        lanes = slice(128 * l, 128 * l + 128)
-        r = ref[:, lanes]
-        rest[pl.ds(l, 3, stride=NB), :] = r
-        shift[pl.ds(l, 3, stride=NB), :] = disp[:, lanes]
-        speed[pl.ds(l, 3, stride=NB), :] = vel[:, lanes]
-    wet[...] = mask[...].astype(F32)
-    press[...] = pres[...]
-    slots_rest[...] = jnp.zeros_like(slots_rest)
-    slots_move[...] = jnp.zeros_like(slots_move)
-    chosen = jnp.concatenate([send_v[p : p + 1, :] for p in range(PEERS)], axis=1)
-    block = lax.broadcasted_iota(jnp.int32, (NB, PEERS * CAP), 0)
-    table = jnp.where(chosen == block, 1.0, 0.0)
-    owner[...] = table.astype(BF16)
-    chooser[...] = jnp.transpose(table).astype(BF16)
-
-    def fields(buffer, count):
-        return [buffer[f * NB : (f + 1) * NB, :] for f in range(count)]
+    def gather_blocks(pairs_of_refs):
+        for l in range(NB):
+            for src, dst in pairs_of_refs:
+                dst[pl.ds(l, 3, stride=NB), :] = src[:, 128 * l : 128 * l + 128]
+
+    def fields(buffer):
+        return [buffer[f * NB : (f + 1) * NB, :] for f in range(3)]
 
     def placed():
-        return [r + d for r, d in zip(fields(rest, 3), fields(shift, 3))]
-
-    def remote(src, dst, phase, n, o):
-        return pltpu.make_async_remote_copy(
-            src_ref=src.at[peer[o]],
-            dst_ref=dst.at[s],
-            send_sem=send_sem.at[phase, n],
-            recv_sem=recv_sem.at[phase, n],
-            device_id=(peer[o], u),
-            device_id_type=MESH,
-        )
-
-    def send_row(src, dst, phase, dy):
-        copies = []
-        for n, o in enumerate(OFFSETS):
-            if o[0] == dy and o != (0, 0):
-                copy = remote(src, dst, phase, n, o)
-                copy.start()
-                copies.append(copy)
-        return copies
-
-    def distribute(values, src, dst, phase):
+        return [r + d for r, d in zip(fields(rest), fields(shift))]
+
+    def load_of(pressure):
+        return 0.5 + (0.5 * COUPLING) * (pressure * wet[...])
+
+    def choose(values, dst):
         parts = split(jnp.concatenate(values, axis=1))
-        copies = []
-        for dy in (1, 2, 3, 0):
-            row = (y + dy) % SIDE
-            pick = chooser[pl.ds(pl.multiple_of(row * SIDE * CAP, SIDE * CAP), SIDE * CAP), :]
+        for row in range(SIDE):
+            pick = chooser[row * SIDE * CAP : (row + 1) * SIDE * CAP, :]
             picked = dot(pick, parts[0]) + dot(pick, parts[1]) + dot(pick, parts[2])
             for q in range(SIDE):
                 for f in range(len(values)):
-                    src[row * SIDE + q, pl.ds(f * CAP, CAP), :] = picked[
+                    dst[row * SIDE + q, f * CAP : (f + 1) * CAP, :] = picked[
                         q * CAP : (q + 1) * CAP, f * 128 : (f + 1) * 128
                     ]
-            copies += send_row(src, dst, phase, dy)
-        dst[s] = src[s]
+
+    def send(src, dst, phase):
+        copies = []
+        for n, target in enumerate(targets):
+            copy = pltpu.make_async_remote_copy(
+                src_ref=src.at[target],
+                dst_ref=dst.at[s],
+                send_sem=send_sem.at[phase, n],
+                recv_sem=recv_sem.at[phase, n],
+                device_id=(target, u),
+                device_id_type=MESH,
+            )
+            copy.start()
+            copies.append(copy)
         return copies
 
-    def spread(src, dst, count):
-        @pl.loop(0, PEERS)
-        def _(p):
+    def place(src, dst, p, first, count):
+        for f in range(count):
             for g in range(CAP // 8):
-                for f in range(count):
-                    dst[pl.ds(p * CAP + 8 * g, 8), f, :] = src[p, pl.ds(f * CAP + 8 * g, 8), :]
+                dst[pl.ds(p * CAP + 8 * g, 8), first + f, :] = src[
+                    p, pl.ds(f * CAP + 8 * g, 8), :
+                ]
+
+    def receive(copies, own, src, dst, first, count):
+        place(own, dst, s, first, count)
+        for copy, p in zip(copies, sources):
+            copy.wait_recv()
+            place(src, dst, p, first, count)
 
     def halo(src, n, dev, dst):
         return pltpu.make_async_remote_copy(
             src_ref=src, dst_ref=dst, send_sem=halo_send.at[n], recv_sem=halo_recv.at[n],
             device_id=dev, device_id_type=MESH,
         )
-
-    cells0[0] = pres[...]
-    cells0[1] = wet[...]
-    cells0[2] = cond[...] * wet[...]
-    pl.semaphore_wait(barrier, PEERS - 1 + 2)
-
-    rest_copies = distribute(fields(rest, 3), ref_out, ref_in, 0)
-
-    def load_of(pressure):
-        return 0.5 + (0.5 * COUPLING) * (pressure * wet[...])
-
-    move_copies = distribute(placed() + [load_of(press[...])], mov_out0, mov_in0, 1)
-
-    halos = [
-        halo(cells0.at[:, pl.ds(56, 8)], 0, (down, u), north0),
-        halo(cells0.at[:, pl.ds(0, 8)], 1, (up, u), south0),
-        halo(cells0, 2, (s, right), west0),
-        halo(cells0, 3, (s, left), east0),
-    ]
-    for copy in halos:
-        copy.start()
-
-    for copy in rest_copies:
-        copy.wait_recv()
-    spread(ref_in, slots_rest, 3)
-    flag_copy.wait()
-
-    @pl.loop(0, PAIRS // REST_GROUP)
-    def _(j):
-        rest_group(
-            [j * REST_GROUP + d for d in range(REST_GROUP)], pair_s, slots_rest, flags, c1, c2
-        )
-
-    for copy in move_copies:
-        copy.wait_recv()
 
     rows = lax.broadcasted_iota(jnp.int32, (64, 128), 0)
     lanes = lax.broadcasted_iota(jnp.int32, (64, 128), 1)
@@ -314,9 +278,7 @@
             total = total + face[...] * (around[value] - centre)
         press[...] = centre + FLOW * total
 
-    def pair_forces(mov_in):
-        spread(mov_in, slots_move, 4)
-
+    def pair_forces():
         def members(j):
             return [j * GROUP + d for d in range(GROUP)]
 
@@ -340,26 +302,23 @@
         make(1, groups - 1)
         add(1, groups - 1)
 
-    live = lax.broadcasted_iota(jnp.int32, (2, PAIRS), 1) < count_s[0]
-    named = jnp.where(live, pair_v[...], -1)
-    ends = jnp.concatenate([named[0:1, :], named[1:2, :]], axis=1)
-
     def give_back(src, dst, phase):
+        live = lax.broadcasted_iota(jnp.int32, (2, PAIRS), 1) < count_s[0]
+        named = jnp.where(live, pair_v[...], -1)
+        ends = jnp.concatenate([named[0:1, :], named[1:2, :]], axis=1)
         parts = split(
             jnp.concatenate([on[f * 2 * PAIRS : (f + 1) * 2 * PAIRS, :] for f in range(3)], axis=1)
         )
-        copies = []
-        for dy in (1, 2, 3, 0):
-            row = (y + dy) % SIDE
+        for row in range(SIDE):
             slot = lax.broadcasted_iota(jnp.int32, (SIDE * CAP, 2 * PAIRS), 0) + row * (SIDE * CAP)
             hit = jnp.where(slot == ends, 1.0, 0.0).astype(BF16)
-            total = dot(hit, parts[0]) + dot(hit, parts[1]) + dot(hit, parts[2])
+            total = dot(hit, parts[0]) + dot(hit, parts[1])
             for q in range(SIDE):
                 for f in range(3):
-                    src[row * SIDE + q, pl.ds(f * CAP, CAP), :] = total[
+                    src[row * SIDE + q, f * CAP : (f + 1) * CAP, :] = total[
                         q * CAP : (q + 1) * CAP, f * 128 : (f + 1) * 128
                     ]
-            copies += send_row(src, dst, phase, dy)
+        copies = send(src, dst, phase)
         dst[s] = src[s]
         return copies
 
@@ -374,19 +333,60 @@
             )
         )
         table = owner[...]
-        force = dot(table, parts[0]) + dot(table, parts[1]) + dot(table, parts[2])
+        force = dot(table, parts[0]) + dot(table, parts[1])
         for f in range(3):
             part = slice(f * NB, (f + 1) * NB)
             v = speed[part, :] + (DT * FORCE_SCALE) * force[:, f * 128 : (f + 1) * 128]
             speed[part, :] = v
             shift[part, :] = shift[part, :] + DT * v
 
-    pair_forces(mov_in0)
-    back_copies = give_back(frc_out0, frc_in0, 2)
+    gather_blocks([(ref, rest)])
+    chosen = jnp.concatenate([send_v[p : p + 1, :] for p in range(PEERS)], axis=1)
+    block = lax.broadcasted_iota(jnp.int32, (NB, PEERS * CAP), 0)
+    table = jnp.where(chosen == block, 1.0, 0.0)
+    owner[...] = table.astype(BF16)
+    chooser[...] = jnp.transpose(table).astype(BF16)
+    choose(fields(rest), ref_out)
+    pl.semaphore_wait(barrier, len(ORDER) + 2)
+    rest_copies = send(ref_out, ref_in, 0)
+
+    gather_blocks([(disp, shift), (vel, speed)])
+    wet[...] = mask[...].astype(F32)
+    press[...] = pres[...]
+    choose(placed() + [load_of(press[...])], mov_out0)
+    cells0[0] = pres[...]
+    cells0[1] = wet[...]
+    cells0[2] = cond[...] * wet[...]
+    for copy in rest_copies:
+        copy.wait_send()
+    move_copies = send(mov_out0, mov_in0, 1)
+    halos = [
+        halo(cells0.at[:, pl.ds(56, 8)], 0, (down, u), north0),
+        halo(cells0.at[:, pl.ds(0, 8)], 1, (up, u), south0),
+        halo(cells0, 2, (s, right), west0),
+        halo(cells0, 3, (s, left), east0),
+    ]
+    for copy in halos:
+        copy.start()
+    slots_rest[...] = jnp.zeros_like(slots_rest)
+    slots_move[...] = jnp.zeros_like(slots_move)
+
+    receive(rest_copies, ref_out, ref_in, slots_rest, 0, 3)
+    flag_copy.wait()
+
+    @pl.loop(0, PAIRS // REST_GROUP)
+    def _(j):
+        rest_group(
+            [j * REST_GROUP + d for d in range(REST_GROUP)], pair_s, slots_rest, flags, c1, c2
+        )
+
     for copy in halos:
         copy.wait_recv()
     faces()
     flow(north0[0], south0[0], west0[0], east0[0])
+    choose([load_of(press[...])], load_out)
+    receive(move_copies, mov_out0, mov_in0, slots_move, 0, 4)
+    load_copies = send(load_out, load_in, 3)
     cells1[...] = press[...]
     halos1 = [
         halo(cells1.at[pl.ds(56, 8)], 4, (down, u), north1),
@@ -396,25 +396,29 @@
     ]
     for copy in halos1:
         copy.start()
+
+    pair_forces()
+    back_copies = give_back(frc_out0, frc_in0, 2)
+    receive(load_copies, load_out, load_in, slots_move, 3, 1)
+    for copy in halos1:
+        copy.wait_recv()
+    flow(north1[...], south1[...], west1[...], east1[...])
+    state[6 * NB :, :] = press[...]
     for copy in back_copies:
         copy.wait_recv()
     advance(frc_in0)
 
-    next_copies = distribute(placed() + [load_of(press[...])], mov_out1, mov_in1, 3)
-    for copy in halos1:
-        copy.wait_recv()
-    flow(north1[...], south1[...], west1[...], east1[...])
-    for copy in next_copies:
-        copy.wait_recv()
-    pair_forces(mov_in1)
-    last_copies = give_back(frc_out1, frc_in1, 4)
+    choose(placed(), mov_out1)
+    next_copies = send(mov_out1, mov_in1, 4)
+    receive(next_copies, mov_out1, mov_in1, slots_move, 0, 3)
+    pair_forces()
+    last_copies = give_back(frc_out1, frc_in1, 5)
     for copy in last_copies:
         copy.wait_recv()
     advance(frc_in1)
     state[0 : 3 * NB, :] = shift[...]
     state[3 * NB : 6 * NB, :] = speed[...]
-    state[6 * NB :, :] = press[...]
-    for copies in (rest_copies, move_copies, halos, back_copies, halos1, next_copies, last_copies):
+    for copies in (move_copies, halos, load_copies, halos1, back_copies, next_copies, last_copies):
         for copy in copies:
             copy.wait_send()
 
@@ -434,6 +438,7 @@
     grid = pltpu.VMEM((64, 128), F32)
     three = pltpu.VMEM((3 * NB, 128), F32)
     third = pltpu.VMEM((PEERS, 3 * CAP, 128), F32)
+    first = pltpu.VMEM((PEERS, CAP, 128), F32)
     fourth = pltpu.VMEM((PEERS, 4 * CAP, 128), F32)
     slots = pltpu.VMEM((PEERS * CAP, 8, 128), F32)
     grids = pltpu.VMEM((3, 64, 128), F32)
@@ -456,12 +461,12 @@
             pltpu.VMEM((2, GROUP, 2, 128, 128), BF16),
             pltpu.VMEM((2, GROUP, 2, 16, 128), BF16),
             pltpu.VMEM((2, GROUP, 2, 8, 128), F32),
-            third, third, fourth, fourth, fourth, fourth, third, third, third, third,
+            third, third, fourth, third, fourth, third, third, third, third, third, first, first,
             grids, grid, grids, grids, grid, grid, strips, strips, strip, strip,
             grid, grid, grid, grid, grid, grid,
             pltpu.SemaphoreType.DMA,
-            pltpu.SemaphoreType.DMA((5, PEERS)),
-            pltpu.SemaphoreType.DMA((5, PEERS)),
+            pltpu.SemaphoreType.DMA((6, PEERS)),
+            pltpu.SemaphoreType.DMA((6, PEERS)),
             pltpu.SemaphoreType.DMA((8,)),
             pltpu.SemaphoreType.DMA((8,)),
         ],

time: 108 us -> 98 us (0.907)
  Pallas kernels: 106 us -> 96.4 us
    pallas_call x1, Pallas kernels: 104 us -> 94.6 us  [body(): pl.pallas_call(kernel, out_shape=jax.ShapeDtypeStruct((7 * NB, 128), F32)...]
where the time goes in v3:
time: 98 us; the launch traced here: 97.7 us
  Pallas kernels  96.4 us (98%)
  between operations  1.29 us (1%)
    pallas_call x1, Pallas kernels, body(): pl.pallas_call(kernel, out_shape=jax.ShapeDtypeStruct((7 * NB, 128), F32)...  94.6 us

profile of v3, /device:TPU:96, one launch (start us, length us, event | category | flops | bytes accessed | tf_op | source)
XLA Modules:
  0.0 97.7 jit_solution(11585424871417186696)
XLA Ops:
  1.3 94.6 %shard_map.121.state = f32[448,128]{1,0:T(8,128)} custom-call(s32[2,256]{1,0:T(2,128)} %bitcast.3, s32[1]{0:T(128)S(6)} %copy.13.count_s, f32[3,8192]{1,0:T(4,128)} %ref.1, f32[3,8192]{1,0:T(4,128)} %disp.1, f32[3,8192]{1,0:T(4,128)} %vel.1, f32[64,128]{1,0:T(8,128)} %pres.1, f32[64,128]{1,0:T(8,128)} %cond.1, s32[64,128]{1,0:T(8,128)} %mask.1, ...), custom_call_target="tpu_custom_call" | custom-call | tf_op jit(solution)/shard_map/pallas_call | solution.py:448
  95.9 1.8 %shard_map.122 = (f32[3,8192]{1,0:T(4,128)}, f32[3,8192]{1,0:T(4,128)}, f32[64,128]{1,0:T(8,128)}) custom-call(f32[448,128]{1,0:T(8,128)} %shard_map.121.state), custom_call_target="tpu_custom_call" | custom-call | tf_op jit(solution)/shard_map/pallas_call | solution.py:480

commit v4 on v3

--- a/solution.py
+++ b/solution.py
@@ -24,8 +24,9 @@
 PAIRS = 256
 SIDE = 4
 PEERS = SIDE * SIDE
-GROUP = 8
+GROUP = 16
 REST_GROUP = 16
+NEAR = 8
 ORDER = [
     (0, 1), (1, 0), (0, 3), (3, 0), (1, 1), (3, 3), (1, 3), (3, 1),
     (0, 2), (2, 0), (1, 2), (2, 1), (3, 2), (2, 3), (2, 2),
@@ -135,15 +136,10 @@
     for d in range(len(ks)):
         ca, cb = coords[buffer, d, 0], coords[buffer, d, 1]
         high, low = factor[buffer, d, 0], factor[buffer, d, 1]
-        sums.append(
-            (
-                dot(
-                    jnp.concatenate([cb, cb], axis=1),
-                    jnp.concatenate([high, low], axis=1), 1, 1,
-                ),
-                dot(jnp.concatenate([ca, ca], axis=1), stack([high, low])),
-            )
-        )
+        wide = jnp.concatenate([high, low], axis=1)
+        on_first = dot(wide, jnp.concatenate([cb, cb], axis=1), 1, 1)
+        on_second = dot(ca, wide)
+        sums.append((jnp.transpose(on_first), on_second[:, :128] + on_second[:, 128:]))
     for d, (k, (ga, gb)) in enumerate(zip(ks, sums)):
         ga = ga[0:8] + ga[8:16]
         gb = gb[0:8] + gb[8:16]
@@ -154,15 +150,15 @@
 
 
 def kernel(
-    pair_s, count_s, ref, disp, vel, pres, cond, mask, send_v, pair_v, flags_any,
+    pair_s, count_s, ref_any, disp_any, vel_any, pres_any, cond_any, mask_any, send_any, pair_any, flags_any,
     state,
-    flags, rest, shift, speed, owner, chooser, slots_rest, slots_move, on, c1, c2,
+    ref, disp, vel, pres, cond, mask, send_v, pair_v, flags, rest, shift, speed, chooser, slots_rest, slots_move, on, c1, c2,
     factor, coords, tiles,
     ref_out, ref_in, mov_out0, mov_out1, mov_in0, mov_in1, frc_out0, frc_out1, frc_in0, frc_in1,
     load_out, load_in,
     cells0, cells1, west0, east0, west1, east1, north0, south0, north1, south1,
     face_n, face_s, face_w, face_e, press, wet,
-    flag_sem, send_sem, recv_sem, halo_send, halo_recv,
+    in_sem, send_sem, recv_sem, halo_send, halo_recv,
 ):
     s = lax.axis_index("slab")
     u = lax.axis_index("sub")
@@ -179,13 +175,21 @@
     up, down = (s + slabs - 1) % slabs, (s + 1) % slabs
     left, right = (u + subs - 1) % subs, (u + 1) % subs
 
+    loads = []
+    for n, (src, dst) in enumerate(
+        (
+            (send_any, send_v), (ref_any, ref), (disp_any, disp), (vel_any, vel), (pres_any, pres),
+            (mask_any, mask), (cond_any, cond), (pair_any, pair_v), (flags_any, flags),
+        )
+    ):
+        loads.append(pltpu.make_async_copy(src, dst, in_sem.at[n]))
+        loads[n].start()
+
     barrier = pltpu.get_barrier_semaphore()
     for target in targets:
         pl.semaphore_signal(barrier, inc=1, device_id=(target, u), device_id_type=MESH)
     for v in (left, right):
         pl.semaphore_signal(barrier, inc=1, device_id=(s, v), device_id_type=MESH)
-    flag_copy = pltpu.make_async_copy(flags_any, flags, flag_sem)
-    flag_copy.start()
 
     def gather_blocks(pairs_of_refs):
         for l in range(NB):
@@ -201,31 +205,47 @@
     def load_of(pressure):
         return 0.5 + (0.5 * COUPLING) * (pressure * wet[...])
 
-    def choose(values, dst):
-        parts = split(jnp.concatenate(values, axis=1))
-        for row in range(SIDE):
-            pick = chooser[row * SIDE * CAP : (row + 1) * SIDE * CAP, :]
-            picked = dot(pick, parts[0]) + dot(pick, parts[1]) + dot(pick, parts[2])
-            for q in range(SIDE):
-                for f in range(len(values)):
-                    dst[row * SIDE + q, f * CAP : (f + 1) * CAP, :] = picked[
-                        q * CAP : (q + 1) * CAP, f * 128 : (f + 1) * 128
-                    ]
-
-    def send(src, dst, phase):
+    def start(src, dst, phase, part):
         copies = []
-        for n, target in enumerate(targets):
+        for n in part:
             copy = pltpu.make_async_remote_copy(
-                src_ref=src.at[target],
+                src_ref=src.at[targets[n]],
                 dst_ref=dst.at[s],
                 send_sem=send_sem.at[phase, n],
                 recv_sem=recv_sem.at[phase, n],
-                device_id=(target, u),
+                device_id=(targets[n], u),
                 device_id_type=MESH,
             )
             copy.start()
             copies.append(copy)
         return copies
+
+    def fill(row, picked, dst, count):
+        for q in range(SIDE):
+            for f in range(count):
+                dst[row * SIDE + q, f * CAP : (f + 1) * CAP, :] = picked[
+                    q * CAP : (q + 1) * CAP, f * 128 : (f + 1) * 128
+                ]
+
+    def by_rows(make_row, src, dst, phase, count, ready=None):
+        copies = []
+        for step in (0, 1, 3, 2):
+            row = (y + step) % SIDE
+            fill(row, make_row(row), src, count)
+            if step == 3:
+                if ready is not None:
+                    ready()
+                copies += start(src, dst, phase, range(NEAR))
+        return copies + start(src, dst, phase, range(NEAR, len(ORDER)))
+
+    def chosen_rows(values):
+        parts = split(jnp.concatenate(values, axis=1))
+
+        def make_row(row):
+            pick = chooser[pl.ds(pl.multiple_of(row * SIDE * CAP, SIDE * CAP), SIDE * CAP), :]
+            return dot(pick, parts[0]) + dot(pick, parts[1]) + dot(pick, parts[2])
+
+        return make_row
 
     def place(src, dst, p, first, count):
         for f in range(count):
@@ -309,57 +329,56 @@
         parts = split(
             jnp.concatenate([on[f * 2 * PAIRS : (f + 1) * 2 * PAIRS, :] for f in range(3)], axis=1)
         )
-        for row in range(SIDE):
+
+        def make_row(row):
             slot = lax.broadcasted_iota(jnp.int32, (SIDE * CAP, 2 * PAIRS), 0) + row * (SIDE * CAP)
             hit = jnp.where(slot == ends, 1.0, 0.0).astype(BF16)
-            total = dot(hit, parts[0]) + dot(hit, parts[1])
-            for q in range(SIDE):
-                for f in range(3):
-                    src[row * SIDE + q, f * CAP : (f + 1) * CAP, :] = total[
-                        q * CAP : (q + 1) * CAP, f * 128 : (f + 1) * 128
-                    ]
-        copies = send(src, dst, phase)
-        dst[s] = src[s]
-        return copies
-
-    def advance(frc_in):
-        parts = split(
-            jnp.concatenate(
-                [
-                    frc_in[:, f * CAP : (f + 1) * CAP, :].reshape(PEERS * CAP, 128)
-                    for f in range(3)
-                ],
-                axis=1,
-            )
-        )
-        table = owner[...]
-        force = dot(table, parts[0]) + dot(table, parts[1])
+            return dot(hit, parts[0]) + dot(hit, parts[1])
+
+        return by_rows(make_row, src, dst, phase, 3)
+
+    def force_from(src, p):
+        parts = split(jnp.concatenate([src[p, f * CAP : (f + 1) * CAP, :] for f in range(3)], axis=1))
+        pick = chooser[pl.ds(pl.multiple_of(p * CAP, CAP), CAP), :]
+        return dot(pick, parts[0], 0, 0) + dot(pick, parts[1], 0, 0)
+
+    def advance(copies, own, src):
+        force = force_from(own, s)
+        for copy, p in zip(copies, sources):
+            copy.wait_recv()
+            force = force + force_from(src, p)
         for f in range(3):
             part = slice(f * NB, (f + 1) * NB)
             v = speed[part, :] + (DT * FORCE_SCALE) * force[:, f * 128 : (f + 1) * 128]
             speed[part, :] = v
             shift[part, :] = shift[part, :] + DT * v
 
+    for copy in loads[:2]:
+        copy.wait()
     gather_blocks([(ref, rest)])
     chosen = jnp.concatenate([send_v[p : p + 1, :] for p in range(PEERS)], axis=1)
     block = lax.broadcasted_iota(jnp.int32, (NB, PEERS * CAP), 0)
     table = jnp.where(chosen == block, 1.0, 0.0)
-    owner[...] = table.astype(BF16)
     chooser[...] = jnp.transpose(table).astype(BF16)
-    choose(fields(rest), ref_out)
-    pl.semaphore_wait(barrier, len(ORDER) + 2)
-    rest_copies = send(ref_out, ref_in, 0)
-
+    rest_copies = by_rows(
+        chosen_rows(fields(rest)), ref_out, ref_in, 0, 3,
+        lambda: pl.semaphore_wait(barrier, len(ORDER) + 2),
+    )
+
+    for copy in loads[2:7]:
+        copy.wait()
     gather_blocks([(disp, shift), (vel, speed)])
     wet[...] = mask[...].astype(F32)
     press[...] = pres[...]
-    choose(placed() + [load_of(press[...])], mov_out0)
+    make_row = chosen_rows(placed() + [load_of(press[...])])
+    for row in range(SIDE):
+        fill(row, make_row(row), mov_out0, 4)
     cells0[0] = pres[...]
     cells0[1] = wet[...]
     cells0[2] = cond[...] * wet[...]
     for copy in rest_copies:
         copy.wait_send()
-    move_copies = send(mov_out0, mov_in0, 1)
+    move_copies = start(mov_out0, mov_in0, 1, range(len(ORDER)))
     halos = [
         halo(cells0.at[:, pl.ds(56, 8)], 0, (down, u), north0),
         halo(cells0.at[:, pl.ds(0, 8)], 1, (up, u), south0),
@@ -372,7 +391,8 @@
     slots_move[...] = jnp.zeros_like(slots_move)
 
     receive(rest_copies, ref_out, ref_in, slots_rest, 0, 3)
-    flag_copy.wait()
+    for copy in loads[7:]:
+        copy.wait()
 
     @pl.loop(0, PAIRS // REST_GROUP)
     def _(j):
@@ -384,9 +404,11 @@
         copy.wait_recv()
     faces()
     flow(north0[0], south0[0], west0[0], east0[0])
-    choose([load_of(press[...])], load_out)
+    make_row = chosen_rows([load_of(press[...])])
+    for row in range(SIDE):
+        fill(row, make_row(row), load_out, 1)
     receive(move_copies, mov_out0, mov_in0, slots_move, 0, 4)
-    load_copies = send(load_out, load_in, 3)
+    load_copies = start(load_out, load_in, 3, range(len(ORDER)))
     cells1[...] = press[...]
     halos1 = [
         halo(cells1.at[pl.ds(56, 8)], 4, (down, u), north1),
@@ -404,18 +426,13 @@
         copy.wait_recv()
     flow(north1[...], south1[...], west1[...], east1[...])
     state[6 * NB :, :] = press[...]
-    for copy in back_copies:
-        copy.wait_recv()
-    advance(frc_in0)
-
-    choose(placed(), mov_out1)
-    next_copies = send(mov_out1, mov_in1, 4)
+    advance(back_copies, frc_out0, frc_in0)
+
+    next_copies = by_rows(chosen_rows(placed()), mov_out1, mov_in1, 4, 3)
     receive(next_copies, mov_out1, mov_in1, slots_move, 0, 3)
     pair_forces()
     last_copies = give_back(frc_out1, frc_in1, 5)
-    for copy in last_copies:
-        copy.wait_recv()
-    advance(frc_in1)
+    advance(last_copies, frc_out1, frc_in1)
     state[0 : 3 * NB, :] = shift[...]
     state[3 * NB : 6 * NB, :] = speed[...]
     for copies in (move_copies, halos, load_copies, halos1, back_copies, next_copies, last_copies):
@@ -436,6 +453,8 @@
     smem = pl.BlockSpec(memory_space=pltpu.SMEM)
     pairs = pair_list.T
     grid = pltpu.VMEM((64, 128), F32)
+    whole = pltpu.VMEM((64, 128), jnp.int32)
+    wide = pltpu.VMEM((3, NB * 128), F32)
     three = pltpu.VMEM((3 * NB, 128), F32)
     third = pltpu.VMEM((PEERS, 3 * CAP, 128), F32)
     first = pltpu.VMEM((PEERS, CAP, 128), F32)
@@ -448,12 +467,12 @@
     state = pl.pallas_call(
         kernel,
         out_shape=jax.ShapeDtypeStruct((7 * NB, 128), F32),
-        in_specs=[smem, smem] + [vmem] * 8 + [pl.BlockSpec(memory_space=pl.ANY)],
+        in_specs=[smem, smem] + [pl.BlockSpec(memory_space=pl.ANY)] * 9,
         out_specs=vmem,
         scratch_shapes=[
+            wide, wide, wide, grid, grid, whole, pltpu.VMEM((PEERS, CAP), jnp.int32), pltpu.VMEM((2, PAIRS), jnp.int32),
             pltpu.VMEM((10, PAIRS, 128), jnp.int32),
             three, three, three,
-            pltpu.VMEM((NB, PEERS * CAP), BF16),
             pltpu.VMEM((PEERS * CAP, NB), BF16),
             slots, slots,
             pltpu.VMEM((3 * 2 * PAIRS, 128), F32),
@@ -464,7 +483,7 @@
             third, third, fourth, third, fourth, third, third, third, third, third, first, first,
             grids, grid, grids, grids, grid, grid, strips, strips, strip, strip,
             grid, grid, grid, grid, grid, grid,
-            pltpu.SemaphoreType.DMA,
+            pltpu.SemaphoreType.DMA((9,)),
             pltpu.SemaphoreType.DMA((6, PEERS)),
             pltpu.SemaphoreType.DMA((6, PEERS)),
             pltpu.SemaphoreType.DMA((8,)),

time: 98 us -> 94.6 us (0.965)
  Pallas kernels: 96.4 us -> 92.3 us
    pallas_call x1, Pallas kernels: 94.6 us -> 90.5 us  [body(): pl.pallas_call(kernel, out_shape=jax.ShapeDtypeStruct((7 * NB, 128), F32)...]
where the time goes in v4:
time: 94.6 us; the launch traced here: 93.6 us
  Pallas kernels  92.3 us (98%)
  between operations  1.29 us (1%)
    pallas_call x1, Pallas kernels, body(): pl.pallas_call(kernel, out_shape=jax.ShapeDtypeStruct((7 * NB, 128), F32)...  90.5 us

profile of v4, /device:TPU:96, one launch (start us, length us, event | category | flops | bytes accessed | tf_op | source)
XLA Modules:
  0.0 93.6 jit_solution(4825429041021861538)
XLA Ops:
  1.3 90.5 %shard_map.121.state = f32[448,128]{1,0:T(8,128)} custom-call(s32[2,256]{1,0:T(2,128)} %bitcast.3, s32[1]{0:T(128)S(6)} %copy.13.count_s, f32[3,8192]{1,0:T(4,128)} %ref_any.1, f32[3,8192]{1,0:T(4,128)} %disp_any.1, f32[3,8192]{1,0:T(4,128)} %vel_any.1, f32[64,128]{1,0:T(8,128)} %pres_any.1, f32[64,128]{1,0:T(8,128)} %cond_any.1, s32[64,128]{1,0:T(8,128)} %mask_any.1, ...), custom_call_target="tpu_custom_call" | custom-call | tf_op jit(solution)/shard_map/pallas_call | solution.py:467
  91.8 1.8 %shard_map.122 = (f32[3,8192]{1,0:T(4,128)}, f32[3,8192]{1,0:T(4,128)}, f32[64,128]{1,0:T(8,128)}) custom-call(f32[448,128]{1,0:T(8,128)} %shard_map.121.state), custom_call_target="tpu_custom_call" | custom-call | tf_op jit(solution)/shard_map/pallas_call | solution.py:499

commit v5 on v4

--- a/solution.py
+++ b/solution.py
@@ -150,9 +150,9 @@
 
 
 def kernel(
-    pair_s, count_s, ref_any, disp_any, vel_any, pres_any, cond_any, mask_any, send_any, pair_any, flags_any,
+    count_any, ref_any, disp_any, vel_any, pres_any, cond_any, mask_any, send_any, pair_any, flags_any,
     state,
-    ref, disp, vel, pres, cond, mask, send_v, pair_v, flags, rest, shift, speed, chooser, slots_rest, slots_move, on, c1, c2,
+    pair_s, count_s, ref, disp, vel, pres, cond, mask, send_v, pair_v, flags, rest, shift, speed, chooser, slots_rest, slots_move, on, c1, c2,
     factor, coords, tiles,
     ref_out, ref_in, mov_out0, mov_out1, mov_in0, mov_in1, frc_out0, frc_out1, frc_in0, frc_in1,
     load_out, load_in,
@@ -179,7 +179,8 @@
     for n, (src, dst) in enumerate(
         (
             (send_any, send_v), (ref_any, ref), (disp_any, disp), (vel_any, vel), (pres_any, pres),
-            (mask_any, mask), (cond_any, cond), (pair_any, pair_v), (flags_any, flags),
+            (mask_any, mask), (cond_any, cond), (pair_any, pair_v), (pair_any, pair_s), (count_any, count_s),
+            (flags_any, flags),
         )
     ):
         loads.append(pltpu.make_async_copy(src, dst, in_sem.at[n]))
@@ -450,7 +451,6 @@
 
 def body(ref_pos, disp, vel, pressure, conductivity, frac_mask, send_list, pair_list, pair_count, bond_flags):
     vmem = pl.BlockSpec(memory_space=pltpu.VMEM)
-    smem = pl.BlockSpec(memory_space=pltpu.SMEM)
     pairs = pair_list.T
     grid = pltpu.VMEM((64, 128), F32)
     whole = pltpu.VMEM((64, 128), jnp.int32)
@@ -467,9 +467,10 @@
     state = pl.pallas_call(
         kernel,
         out_shape=jax.ShapeDtypeStruct((7 * NB, 128), F32),
-        in_specs=[smem, smem] + [pl.BlockSpec(memory_space=pl.ANY)] * 9,
+        in_specs=[pl.BlockSpec(memory_space=pl.ANY)] * 10,
         out_specs=vmem,
         scratch_shapes=[
+            pltpu.SMEM((2, PAIRS), jnp.int32), pltpu.SMEM((1,), jnp.int32),
             wide, wide, wide, grid, grid, whole, pltpu.VMEM((PEERS, CAP), jnp.int32), pltpu.VMEM((2, PAIRS), jnp.int32),
             pltpu.VMEM((10, PAIRS, 128), jnp.int32),
             three, three, three,
@@ -483,7 +484,7 @@
             third, third, fourth, third, fourth, third, third, third, third, third, first, first,
             grids, grid, grids, grids, grid, grid, strips, strips, strip, strip,
             grid, grid, grid, grid, grid, grid,
-            pltpu.SemaphoreType.DMA((9,)),
+            pltpu.SemaphoreType.DMA((11,)),
             pltpu.SemaphoreType.DMA((6, PEERS)),
             pltpu.SemaphoreType.DMA((6, PEERS)),
             pltpu.SemaphoreType.DMA((8,)),
@@ -493,7 +494,7 @@
             collective_id=0, has_side_effects=True, vmem_limit_bytes=58 << 20
         ),
     )(
-        pairs, pair_count, ref_pos, disp, vel, pressure, conductivity, frac_mask, send_list, pairs,
+        pair_count, ref_pos, disp, vel, pressure, conductivity, frac_mask, send_list, pairs,
         bond_flags.transpose(1, 0, 2),
     )
     return pl.pallas_call(

time: 94.6 us -> 95.1 us (level)
  no operation moved by 1% of the time
where the time goes in v5:
time: 95.1 us; the launch traced here: 94.5 us
  Pallas kernels  93.2 us (98%)
  between operations  1.29 us (1%)
    pallas_call x1, Pallas kernels, body(): pl.pallas_call(kernel, out_shape=jax.ShapeDtypeStruct((7 * NB, 128), F32)...  91.4 us

profile of v5, /device:TPU:96, one launch (start us, length us, event | category | flops | bytes accessed | tf_op | source)
XLA Modules:
  0.0 94.5 jit_solution(11129372717910613563)
XLA Ops:
  1.3 91.4 %shard_map.121.state = f32[448,128]{1,0:T(8,128)} custom-call(s32[1]{0:T(128)S(6)} %copy.13.count_any, f32[3,8192]{1,0:T(4,128)} %ref_any.1, f32[3,8192]{1,0:T(4,128)} %disp_any.1, f32[3,8192]{1,0:T(4,128)} %vel_any.1, f32[64,128]{1,0:T(8,128)} %pres_any.1, f32[64,128]{1,0:T(8,128)} %cond_any.1, s32[64,128]{1,0:T(8,128)} %mask_any.1, s32[16,32]{1,0:T(8,128)} %send_any.1, ...), custom_call_target="tpu_custom_call" | custom-call | tf_op jit(solution)/shard_map/pallas_call | solution.py:467
  92.7 1.8 %shard_map.122 = (f32[3,8192]{1,0:T(4,128)}, f32[3,8192]{1,0:T(4,128)}, f32[64,128]{1,0:T(8,128)}) custom-call(f32[448,128]{1,0:T(8,128)} %shard_map.121.state), custom_call_target="tpu_custom_call" | custom-call | tf_op jit(solution)/shard_map/pallas_call | solution.py:500
